TPU v7x, 256 devices: a whole 4x4x8 slice. The times are simulated.
256 devices in a mesh: blk: 16 (over y_hi, x, core), tile: 16 (over y_lo, z).
Axes of the slice: x: 4, y: 4 (y_hi: 2, y_lo: 2; y = y_hi * 2 + y_lo), z: 8, core: 2. Of those that a mesh axis runs over, the one named last changes fastest.
Arguments:
- images: bfloat16 [32768, 512], P(('blk', 'tile')), may hold values from -6 to 6
- texts: bfloat16 [32768, 512], P(('blk', 'tile')), may hold values from -6 to 6
- teacher_codes: bfloat16 [32768, 16, 2048], P('blk', None, 'tile'), may hold values from -4 to 4
- teacher_scales: float32 [256, 16, 16], P('blk', None, 'tile'), may hold values from 0.5 to 4
- student_logit_scale: float32 [1], replicated, may hold values from 2 to 6
- logit_bias: float32 [1], replicated, may hold values from -3 to 0
Outputs:
- grad_images: float32 [32768, 512], P(('blk', 'tile'))
- grad_texts: float32 [32768, 512], P(('blk', 'tile'))
All inputs are finite; a program needn't handle non-finite values.
Results may differ from a plain program's by a relative error of at most 0.0044.
Values may be sent and summed in bfloat16 or wider, within the bound.
A program may use at most 128 MiB of HBM per device.

v0:
```python
import jax
import jax.numpy as jnp
from jax import lax
from jax.sharding import PartitionSpec as P

epsilon = 1e-06


def from_behind(block, axis, distance):
    devices = range(lax.axis_size(axis))
    route = [((i - distance) % len(devices), i) for i in devices]
    return lax.ppermute(block, axis, route)


def unit_rows(embedded):
    values = embedded.astype(jnp.float32)
    magnitude = jnp.sqrt(jnp.sum(values * values, axis=-1, keepdims=True) + epsilon)
    return (values / magnitude, magnitude)


def unit_grad(grad_unit, unit_vectors, magnitude):
    inner = jnp.sum(unit_vectors * grad_unit, axis=-1, keepdims=True)
    return (grad_unit - unit_vectors * inner) / magnitude


def send_home(ledger, steps_back):
    if steps_back == 0:
        return ledger
    return from_behind(ledger, "blk", steps_back)


def shards(images, texts, teacher_codes, teacher_scales, student_logit_scale, logit_bias):
    cycle_size = lax.axis_size("blk")
    cycle_index = lax.axis_index("blk")
    image_unit, image_norm = unit_rows(images)
    text_unit, text_norm = unit_rows(texts)
    own_texts = text_unit.astype(jnp.bfloat16)
    every_img = lax.all_gather(image_unit.astype(jnp.bfloat16), "tile", axis=0, tiled=True)
    softness_level = student_logit_scale[0]
    offset_term = logit_bias[0]
    image_count, feature_count = every_img.shape
    row_count = own_texts.shape[0]
    tile_rows = teacher_scales.shape[0]
    tile_cols = teacher_scales.shape[2]

    def pair_step(text_rows, column, gradient_picture):
        pair_scores = lax.dot_general(
            every_img, text_rows, (((1,), (1,)), ((), ())), preferred_element_type=jnp.float32
        )
        student_model = softness_level * pair_scores + offset_term
        code_block = lax.dynamic_index_in_dim(teacher_codes, column, 1, keepdims=False)
        scale_block = lax.dynamic_index_in_dim(teacher_scales, column, 1, keepdims=False)
        teacher = code_block.astype(jnp.float32).reshape(
            tile_rows, image_count // tile_rows, tile_cols, row_count // tile_cols
        )
        teacher = (teacher * scale_block[:, None, :, None]).reshape(image_count, row_count)
        pair_weight = (jax.nn.sigmoid(student_model) - jax.nn.sigmoid(teacher)).astype(jnp.bfloat16)
        gradient_picture = gradient_picture + softness_level * jnp.dot(
            pair_weight, text_rows, preferred_element_type=jnp.float32
        )
        caption_slice = softness_level * lax.dot_general(
            pair_weight, every_img, (((0,), (0,)), ((), ())), preferred_element_type=jnp.float32
        )
        return (gradient_picture, caption_slice)

    gradient_picture, opening = pair_step(
        own_texts, cycle_index, jnp.zeros((image_count, feature_count), jnp.float32)
    )

    def settle(ledger, caption_slice):
        return ledger + caption_slice

    def carry_forward(ledger):
        return from_behind(ledger, "blk", 1)

    ledger_ahead = opening

    def forward_turn(turn_index, loop_state):
        grad_now, text_rows, ledger = loop_state
        text_rows = from_behind(text_rows, "blk", 1)
        ledger = carry_forward(ledger)
        column = (cycle_index - turn_index) % cycle_size
        grad_now, caption_slice = pair_step(text_rows, column, grad_now)
        return (grad_now, text_rows, settle(ledger, caption_slice))

    gradient_picture, forward_rows, ledger_ahead = lax.fori_loop(
        1, cycle_size, forward_turn, (gradient_picture, own_texts, ledger_ahead)
    )
    forward_steps = cycle_size - 1
    grad_text_unit = send_home(ledger_ahead, (cycle_size - forward_steps) % cycle_size)
    grad_image_unit = lax.psum_scatter(gradient_picture, "tile", scatter_dimension=0, tiled=True)
    return (
        unit_grad(grad_image_unit, image_unit, image_norm),
        unit_grad(grad_text_unit, text_unit, text_norm),
    )


def solution(mesh):
    in_specs = (
        P(("blk", "tile"), None),
        P(("blk", "tile"), None),
        P("blk", None, "tile"),
        P("blk", None, "tile"),
        P(),
        P(),
    )
    out_specs = (P(("blk", "tile"), None), P(("blk", "tile"), None))
    return jax.shard_map(shards, mesh=mesh, in_specs=in_specs, out_specs=out_specs, check_vma=False)
```

profile of v0, /device:TPU:2, one launch (start us, length us, event | category | flops | bytes accessed | tf_op | source)
XLA Modules:
  0.0 399.3 jit_solution(15515538781942439000)
XLA Ops:
  10.7 8.8 %copy.11 = bf16[2048,16,128]{2,0,1:T(8,128)(2,1)} copy(bf16[2048,16,128]{2,1,0:T(8,128)(2,1)} %param.10) | data formatting | bytes 16777216 | tf_op args[2]
  20.8 64.1 %all-gather.2.cloned.1.call-done = bf16[2048,512]{1,0:T(8,128)(2,1)} async-done(((bf16[128,512]{1,0:T(8,128)(2,1)}), bf16[2048,512]{1,0:T(8,128)(2,1)}) %all-gather.2.cloned.1.call-update) | async-done | bytes 2097168 | tf_op jit(solution)/shard_map/all_gather | solution.py:38
  84.9 2.4 fusion.18
  87.4 2.7 convolution_multiply_fusion.2
  90.5 211.4 %while.19 = (s32[]{:T(128)}, f32[2048,512]{1,0:T(8,128)}, bf16[128,512]{1,0:T(8,128)(2,1)S(1)}, f32[128,512]{1,0:T(8,128)S(1)}, f32[]{:T(128)}, /*index=5*/bf16[...) while((s32[]{:T(128)}, f32[2048,512]{1,0:T(8,128)}, ...), condition=%wide.region_3.4_spmd, body=%wide.region_2.3_spmd.sunk | while | flops 810680320 | bytes 50872952 | solution.py:86
  92.3 2.7 collective-permute-done
  95.0 3.4 fusion.53
  103.5 2.7 collective-permute-done
  106.3 3.4 fusion.53
  114.8 2.7 collective-permute-done
  117.6 3.4 fusion.53
  126.1 5.3 %collective-permute-done = bf16[128,512]{1,0:T(8,128)(2,1)S(1)} collective-permute-done((bf16[128,512]{1,0:T(8,128)(2,1)S(1)}, bf16[128,512]{1,0:T(8,128)(2,1)S(1)}, u32[]{:S(2)}, u32[]{:S(2)}) %collective-permute-start) | collective-permute-done | bytes 131104 | tf_op jit(solution)/shard_map/while/body/eval_jaxpr/ppermute | solution.py:12
  131.4 3.4 fusion.53
  138.3 1.7 collective-permute-start.1
  140.0 6.2 %collective-permute-done = bf16[128,512]{1,0:T(8,128)(2,1)S(1)} collective-permute-done((bf16[128,512]{1,0:T(8,128)(2,1)S(1)}, bf16[128,512]{1,0:T(8,128)(2,1)S(1)}, u32[]{:S(2)}, u32[]{:S(2)}) %collective-permute-start) | collective-permute-done | bytes 131104 | tf_op jit(solution)/shard_map/while/body/eval_jaxpr/ppermute | solution.py:12
  146.3 3.4 fusion.53
  153.1 1.7 collective-permute-start.1
  154.9 6.2 %collective-permute-done = bf16[128,512]{1,0:T(8,128)(2,1)S(1)} collective-permute-done((bf16[128,512]{1,0:T(8,128)(2,1)S(1)}, bf16[128,512]{1,0:T(8,128)(2,1)S(1)}, u32[]{:S(2)}, u32[]{:S(2)}) %collective-permute-start) | collective-permute-done | bytes 131104 | tf_op jit(solution)/shard_map/while/body/eval_jaxpr/ppermute | solution.py:12
  161.2 3.4 fusion.53
  168.0 1.7 collective-permute-start.1
  169.8 6.2 %collective-permute-done = bf16[128,512]{1,0:T(8,128)(2,1)S(1)} collective-permute-done((bf16[128,512]{1,0:T(8,128)(2,1)S(1)}, bf16[128,512]{1,0:T(8,128)(2,1)S(1)}, u32[]{:S(2)}, u32[]{:S(2)}) %collective-permute-start) | collective-permute-done | bytes 131104 | tf_op jit(solution)/shard_map/while/body/eval_jaxpr/ppermute | solution.py:12
  176.0 3.4 fusion.53
  182.9 1.7 collective-permute-start.1
  184.7 6.2 %collective-permute-done = bf16[128,512]{1,0:T(8,128)(2,1)S(1)} collective-permute-done((bf16[128,512]{1,0:T(8,128)(2,1)S(1)}, bf16[128,512]{1,0:T(8,128)(2,1)S(1)}, u32[]{:S(2)}, u32[]{:S(2)}) %collective-permute-start) | collective-permute-done | bytes 131104 | tf_op jit(solution)/shard_map/while/body/eval_jaxpr/ppermute | solution.py:12
  190.9 3.4 fusion.53
  197.8 1.7 collective-permute-start.1
  199.5 6.2 %collective-permute-done = bf16[128,512]{1,0:T(8,128)(2,1)S(1)} collective-permute-done((bf16[128,512]{1,0:T(8,128)(2,1)S(1)}, bf16[128,512]{1,0:T(8,128)(2,1)S(1)}, u32[]{:S(2)}, u32[]{:S(2)}) %collective-permute-start) | collective-permute-done | bytes 131104 | tf_op jit(solution)/shard_map/while/body/eval_jaxpr/ppermute | solution.py:12
  205.8 3.4 fusion.53
  212.6 1.7 collective-permute-start.1
  214.4 6.2 %collective-permute-done = bf16[128,512]{1,0:T(8,128)(2,1)S(1)} collective-permute-done((bf16[128,512]{1,0:T(8,128)(2,1)S(1)}, bf16[128,512]{1,0:T(8,128)(2,1)S(1)}, u32[]{:S(2)}, u32[]{:S(2)}) %collective-permute-start) | collective-permute-done | bytes 131104 | tf_op jit(solution)/shard_map/while/body/eval_jaxpr/ppermute | solution.py:12
  220.7 3.4 fusion.53
  227.5 1.7 collective-permute-start.1
  229.3 6.2 %collective-permute-done = bf16[128,512]{1,0:T(8,128)(2,1)S(1)} collective-permute-done((bf16[128,512]{1,0:T(8,128)(2,1)S(1)}, bf16[128,512]{1,0:T(8,128)(2,1)S(1)}, u32[]{:S(2)}, u32[]{:S(2)}) %collective-permute-start) | collective-permute-done | bytes 131104 | tf_op jit(solution)/shard_map/while/body/eval_jaxpr/ppermute | solution.py:12
  235.5 3.4 fusion.53
  242.4 1.7 collective-permute-start.1
  244.2 6.2 %collective-permute-done = bf16[128,512]{1,0:T(8,128)(2,1)S(1)} collective-permute-done((bf16[128,512]{1,0:T(8,128)(2,1)S(1)}, bf16[128,512]{1,0:T(8,128)(2,1)S(1)}, u32[]{:S(2)}, u32[]{:S(2)}) %collective-permute-start) | collective-permute-done | bytes 131104 | tf_op jit(solution)/shard_map/while/body/eval_jaxpr/ppermute | solution.py:12
  250.4 3.4 fusion.53
  257.3 1.7 collective-permute-start.1
  259.0 6.2 %collective-permute-done = bf16[128,512]{1,0:T(8,128)(2,1)S(1)} collective-permute-done((bf16[128,512]{1,0:T(8,128)(2,1)S(1)}, bf16[128,512]{1,0:T(8,128)(2,1)S(1)}, u32[]{:S(2)}, u32[]{:S(2)}) %collective-permute-start) | collective-permute-done | bytes 131104 | tf_op jit(solution)/shard_map/while/body/eval_jaxpr/ppermute | solution.py:12
  265.3 3.4 fusion.53
  273.9 6.2 %collective-permute-done = bf16[128,512]{1,0:T(8,128)(2,1)S(1)} collective-permute-done((bf16[128,512]{1,0:T(8,128)(2,1)S(1)}, bf16[128,512]{1,0:T(8,128)(2,1)S(1)}, u32[]{:S(2)}, u32[]{:S(2)}) %collective-permute-start) | collective-permute-done | bytes 131104 | tf_op jit(solution)/shard_map/while/body/eval_jaxpr/ppermute | solution.py:12
  280.2 3.4 fusion.53
  287.0 1.7 collective-permute-start.1
  288.8 6.2 %collective-permute-done = bf16[128,512]{1,0:T(8,128)(2,1)S(1)} collective-permute-done((bf16[128,512]{1,0:T(8,128)(2,1)S(1)}, bf16[128,512]{1,0:T(8,128)(2,1)S(1)}, u32[]{:S(2)}, u32[]{:S(2)}) %collective-permute-start) | collective-permute-done | bytes 131104 | tf_op jit(solution)/shard_map/while/body/eval_jaxpr/ppermute | solution.py:12
  295.1 3.4 fusion.53
  302.0 9.4 %collective-permute-done.2 = f32[128,512]{1,0:T(8,128)S(1)} collective-permute-done((f32[128,512]{1,0:T(8,128)S(1)}, f32[128,512]{1,0:T(8,128)S(1)}, u32[]{:S(2)}, u32[]{:S(2)}) %collective-permute-start.2) | collective-permute-done | bytes 262176 | tf_op jit(solution)/shard_map/ppermute | solution.py:12
  312.4 77.1 %reduce-scatter.2.cloned.1.call-done = f32[128,512]{1,0:T(8,128)} async-done(((f32[2048,512]{1,0:T(8,128)}), f32[128,512]{1,0:T(8,128)}) %reduce-scatter.2.cloned.1.call-update) | async-done | bytes 262160 | tf_op jit(solution)/shard_map/reduce_scatter | solution.py:91
  390.6 1.8 subtract_divide_fusion.1
  (196 shorter events, 66.2 us)
Async XLA Ops:
  7.2 77.8 %all-gather.2.cloned.1.call-start = ((), (), s32[]{:S(2)}) async-start(), calls=%async_computation.1 | async-start | bytes 2228224 | tf_op jit(solution)/shard_map/all_gather | solution.py:38
  9.9 379.6 %reduce-scatter.2.cloned.1.call-start = ((), (), s32[]{:S(2)}) async-start(), calls=%async_computation.2 | async-start | bytes 4456448 | tf_op jit(solution)/shard_map/reduce_scatter | solution.py:91
  10.6 9.5 %copy-start.5 = (f32[16,16,1]{1,2,0:T(1,128)S(1)}, f32[16,16,1]{1,2,0:T(1,128)}, u32[]{:S(2)}) copy-start(f32[16,16,1]{1,2,0:T(1,128)} %param.11) | copy-start | bytes 3076
  10.6 9.8 %copy-start.3 = (bf16[128,512]{1,0:T(8,128)(2,1)S(1)}, bf16[128,512]{1,0:T(8,128)(2,1)}, u32[]{:S(2)}) copy-start(bf16[128,512]{1,0:T(8,128)(2,1)} %param.9) | copy-start | bytes 393220
  90.5 4.5 %collective-permute-start = (bf16[128,512]{1,0:T(8,128)(2,1)S(1)}, bf16[128,512]{1,0:T(8,128)(2,1)S(1)}, u32[]{:S(2)}, u32[]{:S(2)}) collective-permute-start(bf16[128,512]{1,0:T(8,128)(2,1)S(1)} %get-tuple-element.365), channel_id=1, source_target_pairs={{240,0},{0,16},{16,32},{32,48},{48,64},{64,80},{80,96},{96,112},{1... | collective-permute-start | bytes 393224 | tf_op jit(solution)/shard_map/while/body/eval_jaxpr/ppermute | solution.py:12
  90.6 9.3 %collective-permute-start.1 = (f32[128,512]{1,0:T(8,128)S(1)}, f32[128,512]{1,0:T(8,128)S(1)}, u32[]{:S(2)}, u32[]{:S(2)}) collective-permute-start(f32[128,512]{1,0:T(8,128)S(1)} %get-tuple-element.366), channel_id=1, source_target_pairs={{240,0},{0,16},{16,32},{32,48},{48,64},{64,80},{80,96},{96,112},{1... | collective-permute-start | bytes 786440 | tf_op jit(solution)/shard_map/while/body/eval_jaxpr/ppermute | solution.py:12
  101.9 4.4 %collective-permute-start = (bf16[128,512]{1,0:T(8,128)(2,1)S(1)}, bf16[128,512]{1,0:T(8,128)(2,1)S(1)}, u32[]{:S(2)}, u32[]{:S(2)}) collective-permute-start(bf16[128,512]{1,0:T(8,128)(2,1)S(1)} %get-tuple-element.365), channel_id=1, source_target_pairs={{240,0},{0,16},{16,32},{32,48},{48,64},{64,80},{80,96},{96,112},{1... | collective-permute-start | bytes 393224 | tf_op jit(solution)/shard_map/while/body/eval_jaxpr/ppermute | solution.py:12
  101.9 9.3 %collective-permute-start.1 = (f32[128,512]{1,0:T(8,128)S(1)}, f32[128,512]{1,0:T(8,128)S(1)}, u32[]{:S(2)}, u32[]{:S(2)}) collective-permute-start(f32[128,512]{1,0:T(8,128)S(1)} %get-tuple-element.366), channel_id=1, source_target_pairs={{240,0},{0,16},{16,32},{32,48},{48,64},{64,80},{80,96},{96,112},{1... | collective-permute-start | bytes 786440 | tf_op jit(solution)/shard_map/while/body/eval_jaxpr/ppermute | solution.py:12
  113.1 4.4 %collective-permute-start = (bf16[128,512]{1,0:T(8,128)(2,1)S(1)}, bf16[128,512]{1,0:T(8,128)(2,1)S(1)}, u32[]{:S(2)}, u32[]{:S(2)}) collective-permute-start(bf16[128,512]{1,0:T(8,128)(2,1)S(1)} %get-tuple-element.365), channel_id=1, source_target_pairs={{240,0},{0,16},{16,32},{32,48},{48,64},{64,80},{80,96},{96,112},{1... | collective-permute-start | bytes 393224 | tf_op jit(solution)/shard_map/while/body/eval_jaxpr/ppermute | solution.py:12
  113.1 9.3 %collective-permute-start.1 = (f32[128,512]{1,0:T(8,128)S(1)}, f32[128,512]{1,0:T(8,128)S(1)}, u32[]{:S(2)}, u32[]{:S(2)}) collective-permute-start(f32[128,512]{1,0:T(8,128)S(1)} %get-tuple-element.366), channel_id=1, source_target_pairs={{240,0},{0,16},{16,32},{32,48},{48,64},{64,80},{80,96},{96,112},{1... | collective-permute-start | bytes 786440 | tf_op jit(solution)/shard_map/while/body/eval_jaxpr/ppermute | solution.py:12
  124.4 7.0 %collective-permute-start = (bf16[128,512]{1,0:T(8,128)(2,1)S(1)}, bf16[128,512]{1,0:T(8,128)(2,1)S(1)}, u32[]{:S(2)}, u32[]{:S(2)}) collective-permute-start(bf16[128,512]{1,0:T(8,128)(2,1)S(1)} %get-tuple-element.365), channel_id=1, source_target_pairs={{240,0},{0,16},{16,32},{32,48},{48,64},{64,80},{80,96},{96,112},{1... | collective-permute-start | bytes 393224 | tf_op jit(solution)/shard_map/while/body/eval_jaxpr/ppermute | solution.py:12
  124.4 11.9 %collective-permute-start.1 = (f32[128,512]{1,0:T(8,128)S(1)}, f32[128,512]{1,0:T(8,128)S(1)}, u32[]{:S(2)}, u32[]{:S(2)}) collective-permute-start(f32[128,512]{1,0:T(8,128)S(1)} %get-tuple-element.366), channel_id=1, source_target_pairs={{240,0},{0,16},{16,32},{32,48},{48,64},{64,80},{80,96},{96,112},{1... | collective-permute-start | bytes 786440 | tf_op jit(solution)/shard_map/while/body/eval_jaxpr/ppermute | solution.py:12
  131.4 3.4 copy-start
  138.3 8.0 %collective-permute-start = (bf16[128,512]{1,0:T(8,128)(2,1)S(1)}, bf16[128,512]{1,0:T(8,128)(2,1)S(1)}, u32[]{:S(2)}, u32[]{:S(2)}) collective-permute-start(bf16[128,512]{1,0:T(8,128)(2,1)S(1)} %get-tuple-element.365), channel_id=1, source_target_pairs={{240,0},{0,16},{16,32},{32,48},{48,64},{64,80},{80,96},{96,112},{1... | collective-permute-start | bytes 393224 | tf_op jit(solution)/shard_map/while/body/eval_jaxpr/ppermute | solution.py:12
  138.3 12.9 %collective-permute-start.1 = (f32[128,512]{1,0:T(8,128)S(1)}, f32[128,512]{1,0:T(8,128)S(1)}, u32[]{:S(2)}, u32[]{:S(2)}) collective-permute-start(f32[128,512]{1,0:T(8,128)S(1)} %get-tuple-element.366), channel_id=1, source_target_pairs={{240,0},{0,16},{16,32},{32,48},{48,64},{64,80},{80,96},{96,112},{1... | collective-permute-start | bytes 786440 | tf_op jit(solution)/shard_map/while/body/eval_jaxpr/ppermute | solution.py:12
  146.3 3.4 copy-start
  153.1 8.0 %collective-permute-start = (bf16[128,512]{1,0:T(8,128)(2,1)S(1)}, bf16[128,512]{1,0:T(8,128)(2,1)S(1)}, u32[]{:S(2)}, u32[]{:S(2)}) collective-permute-start(bf16[128,512]{1,0:T(8,128)(2,1)S(1)} %get-tuple-element.365), channel_id=1, source_target_pairs={{240,0},{0,16},{16,32},{32,48},{48,64},{64,80},{80,96},{96,112},{1... | collective-permute-start | bytes 393224 | tf_op jit(solution)/shard_map/while/body/eval_jaxpr/ppermute | solution.py:12
  153.1 12.9 %collective-permute-start.1 = (f32[128,512]{1,0:T(8,128)S(1)}, f32[128,512]{1,0:T(8,128)S(1)}, u32[]{:S(2)}, u32[]{:S(2)}) collective-permute-start(f32[128,512]{1,0:T(8,128)S(1)} %get-tuple-element.366), channel_id=1, source_target_pairs={{240,0},{0,16},{16,32},{32,48},{48,64},{64,80},{80,96},{96,112},{1... | collective-permute-start | bytes 786440 | tf_op jit(solution)/shard_map/while/body/eval_jaxpr/ppermute | solution.py:12
  161.2 3.4 copy-start
  168.0 8.0 %collective-permute-start = (bf16[128,512]{1,0:T(8,128)(2,1)S(1)}, bf16[128,512]{1,0:T(8,128)(2,1)S(1)}, u32[]{:S(2)}, u32[]{:S(2)}) collective-permute-start(bf16[128,512]{1,0:T(8,128)(2,1)S(1)} %get-tuple-element.365), channel_id=1, source_target_pairs={{240,0},{0,16},{16,32},{32,48},{48,64},{64,80},{80,96},{96,112},{1... | collective-permute-start | bytes 393224 | tf_op jit(solution)/shard_map/while/body/eval_jaxpr/ppermute | solution.py:12
  168.0 12.9 %collective-permute-start.1 = (f32[128,512]{1,0:T(8,128)S(1)}, f32[128,512]{1,0:T(8,128)S(1)}, u32[]{:S(2)}, u32[]{:S(2)}) collective-permute-start(f32[128,512]{1,0:T(8,128)S(1)} %get-tuple-element.366), channel_id=1, source_target_pairs={{240,0},{0,16},{16,32},{32,48},{48,64},{64,80},{80,96},{96,112},{1... | collective-permute-start | bytes 786440 | tf_op jit(solution)/shard_map/while/body/eval_jaxpr/ppermute | solution.py:12
  176.0 3.4 copy-start
  182.9 8.0 %collective-permute-start = (bf16[128,512]{1,0:T(8,128)(2,1)S(1)}, bf16[128,512]{1,0:T(8,128)(2,1)S(1)}, u32[]{:S(2)}, u32[]{:S(2)}) collective-permute-start(bf16[128,512]{1,0:T(8,128)(2,1)S(1)} %get-tuple-element.365), channel_id=1, source_target_pairs={{240,0},{0,16},{16,32},{32,48},{48,64},{64,80},{80,96},{96,112},{1... | collective-permute-start | bytes 393224 | tf_op jit(solution)/shard_map/while/body/eval_jaxpr/ppermute | solution.py:12
  182.9 12.9 %collective-permute-start.1 = (f32[128,512]{1,0:T(8,128)S(1)}, f32[128,512]{1,0:T(8,128)S(1)}, u32[]{:S(2)}, u32[]{:S(2)}) collective-permute-start(f32[128,512]{1,0:T(8,128)S(1)} %get-tuple-element.366), channel_id=1, source_target_pairs={{240,0},{0,16},{16,32},{32,48},{48,64},{64,80},{80,96},{96,112},{1... | collective-permute-start | bytes 786440 | tf_op jit(solution)/shard_map/while/body/eval_jaxpr/ppermute | solution.py:12
  190.9 3.4 copy-start
  197.8 8.0 %collective-permute-start = (bf16[128,512]{1,0:T(8,128)(2,1)S(1)}, bf16[128,512]{1,0:T(8,128)(2,1)S(1)}, u32[]{:S(2)}, u32[]{:S(2)}) collective-permute-start(bf16[128,512]{1,0:T(8,128)(2,1)S(1)} %get-tuple-element.365), channel_id=1, source_target_pairs={{240,0},{0,16},{16,32},{32,48},{48,64},{64,80},{80,96},{96,112},{1... | collective-permute-start | bytes 393224 | tf_op jit(solution)/shard_map/while/body/eval_jaxpr/ppermute | solution.py:12
  197.8 12.9 %collective-permute-start.1 = (f32[128,512]{1,0:T(8,128)S(1)}, f32[128,512]{1,0:T(8,128)S(1)}, u32[]{:S(2)}, u32[]{:S(2)}) collective-permute-start(f32[128,512]{1,0:T(8,128)S(1)} %get-tuple-element.366), channel_id=1, source_target_pairs={{240,0},{0,16},{16,32},{32,48},{48,64},{64,80},{80,96},{96,112},{1... | collective-permute-start | bytes 786440 | tf_op jit(solution)/shard_map/while/body/eval_jaxpr/ppermute | solution.py:12
  205.8 3.4 copy-start
  212.6 8.0 %collective-permute-start = (bf16[128,512]{1,0:T(8,128)(2,1)S(1)}, bf16[128,512]{1,0:T(8,128)(2,1)S(1)}, u32[]{:S(2)}, u32[]{:S(2)}) collective-permute-start(bf16[128,512]{1,0:T(8,128)(2,1)S(1)} %get-tuple-element.365), channel_id=1, source_target_pairs={{240,0},{0,16},{16,32},{32,48},{48,64},{64,80},{80,96},{96,112},{1... | collective-permute-start | bytes 393224 | tf_op jit(solution)/shard_map/while/body/eval_jaxpr/ppermute | solution.py:12
  212.6 12.9 %collective-permute-start.1 = (f32[128,512]{1,0:T(8,128)S(1)}, f32[128,512]{1,0:T(8,128)S(1)}, u32[]{:S(2)}, u32[]{:S(2)}) collective-permute-start(f32[128,512]{1,0:T(8,128)S(1)} %get-tuple-element.366), channel_id=1, source_target_pairs={{240,0},{0,16},{16,32},{32,48},{48,64},{64,80},{80,96},{96,112},{1... | collective-permute-start | bytes 786440 | tf_op jit(solution)/shard_map/while/body/eval_jaxpr/ppermute | solution.py:12
  220.7 3.4 copy-start
  227.5 8.0 %collective-permute-start = (bf16[128,512]{1,0:T(8,128)(2,1)S(1)}, bf16[128,512]{1,0:T(8,128)(2,1)S(1)}, u32[]{:S(2)}, u32[]{:S(2)}) collective-permute-start(bf16[128,512]{1,0:T(8,128)(2,1)S(1)} %get-tuple-element.365), channel_id=1, source_target_pairs={{240,0},{0,16},{16,32},{32,48},{48,64},{64,80},{80,96},{96,112},{1... | collective-permute-start | bytes 393224 | tf_op jit(solution)/shard_map/while/body/eval_jaxpr/ppermute | solution.py:12
  227.5 12.9 %collective-permute-start.1 = (f32[128,512]{1,0:T(8,128)S(1)}, f32[128,512]{1,0:T(8,128)S(1)}, u32[]{:S(2)}, u32[]{:S(2)}) collective-permute-start(f32[128,512]{1,0:T(8,128)S(1)} %get-tuple-element.366), channel_id=1, source_target_pairs={{240,0},{0,16},{16,32},{32,48},{48,64},{64,80},{80,96},{96,112},{1... | collective-permute-start | bytes 786440 | tf_op jit(solution)/shard_map/while/body/eval_jaxpr/ppermute | solution.py:12
  235.5 3.4 copy-start
  242.4 8.0 %collective-permute-start = (bf16[128,512]{1,0:T(8,128)(2,1)S(1)}, bf16[128,512]{1,0:T(8,128)(2,1)S(1)}, u32[]{:S(2)}, u32[]{:S(2)}) collective-permute-start(bf16[128,512]{1,0:T(8,128)(2,1)S(1)} %get-tuple-element.365), channel_id=1, source_target_pairs={{240,0},{0,16},{16,32},{32,48},{48,64},{64,80},{80,96},{96,112},{1... | collective-permute-start | bytes 393224 | tf_op jit(solution)/shard_map/while/body/eval_jaxpr/ppermute | solution.py:12
  242.4 12.9 %collective-permute-start.1 = (f32[128,512]{1,0:T(8,128)S(1)}, f32[128,512]{1,0:T(8,128)S(1)}, u32[]{:S(2)}, u32[]{:S(2)}) collective-permute-start(f32[128,512]{1,0:T(8,128)S(1)} %get-tuple-element.366), channel_id=1, source_target_pairs={{240,0},{0,16},{16,32},{32,48},{48,64},{64,80},{80,96},{96,112},{1... | collective-permute-start | bytes 786440 | tf_op jit(solution)/shard_map/while/body/eval_jaxpr/ppermute | solution.py:12
  250.4 3.4 copy-start
  257.3 8.0 %collective-permute-start = (bf16[128,512]{1,0:T(8,128)(2,1)S(1)}, bf16[128,512]{1,0:T(8,128)(2,1)S(1)}, u32[]{:S(2)}, u32[]{:S(2)}) collective-permute-start(bf16[128,512]{1,0:T(8,128)(2,1)S(1)} %get-tuple-element.365), channel_id=1, source_target_pairs={{240,0},{0,16},{16,32},{32,48},{48,64},{64,80},{80,96},{96,112},{1... | collective-permute-start | bytes 393224 | tf_op jit(solution)/shard_map/while/body/eval_jaxpr/ppermute | solution.py:12
  257.3 12.9 %collective-permute-start.1 = (f32[128,512]{1,0:T(8,128)S(1)}, f32[128,512]{1,0:T(8,128)S(1)}, u32[]{:S(2)}, u32[]{:S(2)}) collective-permute-start(f32[128,512]{1,0:T(8,128)S(1)} %get-tuple-element.366), channel_id=1, source_target_pairs={{240,0},{0,16},{16,32},{32,48},{48,64},{64,80},{80,96},{96,112},{1... | collective-permute-start | bytes 786440 | tf_op jit(solution)/shard_map/while/body/eval_jaxpr/ppermute | solution.py:12
  265.3 3.4 copy-start
  272.1 8.0 %collective-permute-start = (bf16[128,512]{1,0:T(8,128)(2,1)S(1)}, bf16[128,512]{1,0:T(8,128)(2,1)S(1)}, u32[]{:S(2)}, u32[]{:S(2)}) collective-permute-start(bf16[128,512]{1,0:T(8,128)(2,1)S(1)} %get-tuple-element.365), channel_id=1, source_target_pairs={{240,0},{0,16},{16,32},{32,48},{48,64},{64,80},{80,96},{96,112},{1... | collective-permute-start | bytes 393224 | tf_op jit(solution)/shard_map/while/body/eval_jaxpr/ppermute | solution.py:12
  272.1 12.9 %collective-permute-start.1 = (f32[128,512]{1,0:T(8,128)S(1)}, f32[128,512]{1,0:T(8,128)S(1)}, u32[]{:S(2)}, u32[]{:S(2)}) collective-permute-start(f32[128,512]{1,0:T(8,128)S(1)} %get-tuple-element.366), channel_id=1, source_target_pairs={{240,0},{0,16},{16,32},{32,48},{48,64},{64,80},{80,96},{96,112},{1... | collective-permute-start | bytes 786440 | tf_op jit(solution)/shard_map/while/body/eval_jaxpr/ppermute | solution.py:12
  280.2 3.4 copy-start
  287.0 8.0 %collective-permute-start = (bf16[128,512]{1,0:T(8,128)(2,1)S(1)}, bf16[128,512]{1,0:T(8,128)(2,1)S(1)}, u32[]{:S(2)}, u32[]{:S(2)}) collective-permute-start(bf16[128,512]{1,0:T(8,128)(2,1)S(1)} %get-tuple-element.365), channel_id=1, source_target_pairs={{240,0},{0,16},{16,32},{32,48},{48,64},{64,80},{80,96},{96,112},{1... | collective-permute-start | bytes 393224 | tf_op jit(solution)/shard_map/while/body/eval_jaxpr/ppermute | solution.py:12
  287.0 12.9 %collective-permute-start.1 = (f32[128,512]{1,0:T(8,128)S(1)}, f32[128,512]{1,0:T(8,128)S(1)}, u32[]{:S(2)}, u32[]{:S(2)}) collective-permute-start(f32[128,512]{1,0:T(8,128)S(1)} %get-tuple-element.366), channel_id=1, source_target_pairs={{240,0},{0,16},{16,32},{32,48},{48,64},{64,80},{80,96},{96,112},{1... | collective-permute-start | bytes 786440 | tf_op jit(solution)/shard_map/while/body/eval_jaxpr/ppermute | solution.py:12
  295.0 3.4 copy-start
  301.9 87.6 %copy-start.4 = (bf16[128,512]{1,0:T(8,128)(2,1)S(1)}, bf16[128,512]{1,0:T(8,128)(2,1)}, u32[]{:S(2)}) copy-start(bf16[128,512]{1,0:T(8,128)(2,1)} %param.8) | copy-start | bytes 393220
  301.9 9.5 %collective-permute-start.2 = (f32[128,512]{1,0:T(8,128)S(1)}, f32[128,512]{1,0:T(8,128)S(1)}, u32[]{:S(2)}, u32[]{:S(2)}) collective-permute-start(f32[128,512]{1,0:T(8,128)S(1)} %get-tuple-element.247), channel_id=1, source_target_pairs={{240,0},{0,16},{16,32},{32,48},{48,64},{64,80},{80,96},{96,112},{1... | collective-permute-start | bytes 786440 | tf_op jit(solution)/shard_map/ppermute | solution.py:12
  (19 other events, 42.6 us)
Sparse Core Ops, SparseCore 0:
  10.4 74.5 all-gather.1
  302.0 87.4 reduce-scatter.1
where the time goes:
time: 400 us; the launch traced here: 399 us
  waiting for transfers between devices  233 us (58%)
  matrix products  96 us (24%)
  starting transfers between devices  25.4 us (6%)
  local copies, waits for them, and re-layouts  22 us (6%)
  between operations  15.4 us (4%)
  other arithmetic  6.84 us (2%)
    ppermute x31, waiting for transfers between devices, from_behind(): return lax.ppermute(block, axis, route)  91.5 us
    reduce_scatter x1, waiting for transfers between devices, shards(): lax.psum_scatter(gradient_picture, 'tile', scatter_dimension=0, tiled=True)  77.1 us
    all_gather x1, waiting for transfers between devices, shards(): lax.all_gather(image_unit.astype(jnp.bfloat16), 'tile', axis=0, tiled=True)  64.1 us
    dot_general x16, matrix products, pair_step(): lax.dot_general(every_img, text_rows, (((1,), (1,)), ((), ())), preferred...  53.8 us
    ppermute x31, starting transfers between devices, from_behind(): return lax.ppermute(block, axis, route)  25.3 us
    dot_general x16, matrix products, pair_step(): jnp.dot(pair_weight, text_rows, preferred_element_type=jnp.float32)  23.9 us
    dot_general x16, matrix products, pair_step(): lax.dot_general(pair_weight, every_img, (((0,), (0,)), ((), ())), preferr...  18.2 us
    while x75, local copies, waits for them, and re-layouts  11.7 us
  transfers between devices with their start and end apart: 33, of which 18 were waited for; matrix products, arithmetic and copies ran while one was open for 21% of the time, Pallas kernels for 0%

commit v1 on v0

v1 whole, which is shorter than its diff:
```python
import jax
import jax.numpy as jnp
from jax import lax
from jax.experimental import pallas as pl
from jax.experimental.pallas import tpu as pltpu
from jax.sharding import PartitionSpec as P

EPS = 1e-06
F32 = jnp.float32
BF = jnp.bfloat16
R = 128
E = 512
NZ = 8
NX = 4
NC = 16


def unit_rows(values):
    magnitude = jnp.sqrt(jnp.sum(values * values, axis=-1, keepdims=True) + EPS)
    return values / magnitude, magnitude


def unit_grad(grad_unit, unit_vectors, magnitude):
    inner = jnp.sum(unit_vectors * grad_unit, axis=-1, keepdims=True)
    return (grad_unit - unit_vectors * inner) / magnitude


PLUS = ((4, 0, None), (3, 1, None), (3, 0, 0), (2, 1, 1), (2, 0, 2), (1, 1, 3), (1, 0, 4))
MINUS = ((4, 0, None), (3, 1, None), (3, 0, 0), (2, 1, 1), (2, 0, 2), (1, 0, 4), (1, 1, 3))


def kernel(
    img_ref, txt_ref, codes_ref, scales_ref, scale_ref, bias_ref,
    dimg_ref, dtxt_ref,
    codes, scb, pt, J, T, dI, dT,
    js, jr, ds_, dr, xs, xr, fs, fr,
    codes_sem, jsend, jrecv, tsend, trecv, isend, irecv, dsend, drecv, xsend, xrecv, fsend, frecv,
):
    bi, ti = lax.axis_index("blk"), lax.axis_index("tile")
    h, x, k = bi // 8, (bi // 2) % NX, bi % 2
    l, z = ti // NZ, ti % NZ

    def blk(hh, xx, kk):
        return hh * 8 + ((xx + 8) % NX) * 2 + kk

    def zz(d):
        return (z + d + 16) % NZ

    up, down = {"tile": l * NZ + zz(1)}, {"tile": l * NZ + zz(-1)}
    ylo = {"tile": (1 - l) * NZ + z}
    yhi = {"blk": blk(1 - h, x, k)}
    right, left = {"blk": blk(h, x + 1, k)}, {"blk": blk(h, x - 1, k)}
    core = {"blk": blk(h, x, 1 - k)}

    def codes_copy(r):
        rows = pl.ds(r * R, R)
        return pltpu.make_async_copy(codes_ref.at[rows], codes.at[rows], codes_sem.at[r])

    for r in range(NC):
        codes_copy(r).start()

    barrier = pltpu.get_barrier_semaphore()
    for dev in (up, down, ylo, yhi, right, left, core):
        pl.semaphore_signal(barrier, inc=1, device_id=dev, device_id_type=pl.DeviceIdType.MESH)

    def remote(src, dst, send, recv, dev):
        return pltpu.make_async_remote_copy(
            src_ref=src, dst_ref=dst, send_sem=send, recv_sem=recv, device_id=dev,
            device_id_type=pl.DeviceIdType.MESH,
        )

    def j_copy(i):
        if i == 14:
            return remote(J.at[z, l], J.at[z, l], jsend.at[i], jrecv.at[i], ylo)
        n, sign = (i, 1) if i < 7 else (i - 7, -1)
        if n == 6:
            col = l if sign == 1 else 1 - l
        else:
            col = l if n % 2 == 0 else 1 - l
        spot = J.at[zz(-sign * (n // 2)), col]
        return remote(spot, spot, jsend.at[i], jrecv.at[i], up if sign == 1 else down)

    def j_recv(i):
        j_copy(i).wait_recv()

    def t_copy(i):
        n = i % 3
        if i < 3:
            spot, dev = (T.at[blk(h, x, k)], T.at[blk(1 - h, x, k)], T.at[blk(h, x - 1, k)])[n], right
        elif i < 6:
            spot, dev = (T.at[blk(h, x, k)], T.at[blk(1 - h, x, k)], T.at[blk(1 - h, x + 1, k)])[n], left
        elif i == 6:
            spot, dev = T.at[bi], yhi
        else:
            m = i - 7
            spot, dev = T.at[blk(h if m % 2 == 0 else 1 - h, x + (0, -1, 1, 2)[m // 2], k)], core
        return remote(spot, spot, tsend.at[i], trecv.at[i], dev)

    def t_recv(i):
        t_copy(i).wait_recv()

    img_unit, _ = unit_rows(img_ref[...].astype(F32))
    txt_unit, _ = unit_rows(txt_ref[...].astype(F32))
    J[z, l] = img_unit.astype(BF)
    T[bi] = txt_unit.astype(BF)

    pl.semaphore_wait(barrier, 7)
    for i in (0, 7, 14):
        j_copy(i).start()
    for i in (0, 3, 6, 7):
        t_copy(i).start()

    eye = lax.broadcasted_iota(jnp.int32, (NC, NC), 0) == lax.broadcasted_iota(jnp.int32, (NC, NC), 1)
    for r in range(NC):
        row = jnp.broadcast_to(scales_ref[r], (NC, NC))
        column = jnp.sum(jnp.where(eye, row, 0.0), axis=-1, keepdims=True)
        scb[r] = jnp.broadcast_to(0.5 * column, (NC, R))

    def teacher_rows(r, carry):
        codes_copy(r).wait()
        sc = scb[r]

        def some(g, inner):
            for u in range(16):
                i = r * R + g * 16 + u
                pt[pl.ds(pl.multiple_of(i * NC, NC), NC), :] = jnp.tanh(codes[i].astype(F32) * sc)
            return inner

        return lax.fori_loop(0, R // 16, some, carry)

    lax.fori_loop(0, 8, teacher_rows, 0)
    j_recv(14)
    j_copy(1).start()
    j_copy(8).start()
    t_recv(6)
    for i in (1, 4, 8):
        t_copy(i).start()
    t_recv(0)
    t_copy(9).start()
    t_copy(2).start()
    t_recv(3)
    t_copy(11).start()
    for i in (0, 7):
        j_recv(i)
        j_copy(i + 2).start()
    lax.fori_loop(8, 16, teacher_rows, 0)
    t_recv(1)
    t_copy(10).start()
    t_recv(4)
    t_copy(12).start()
    t_copy(5).start()
    for i in (1, 8):
        j_recv(i)
        j_copy(i + 2).start()
    t_recv(2)
    t_copy(13).start()
    t_recv(5)
    t_copy(14).start()
    for i in range(7, 15):
        t_recv(i)

    half_scale = 0.5 * scale_ref[0]
    half_bias = 0.5 * bias_ref[0]
    dT[...] = jnp.zeros_like(dT)

    def pairs(zb):
        rows = J[zb].reshape(2 * R, E)
        texts = T[...].reshape(NC * R, E)
        score = lax.dot_general(rows, texts, (((1,), (1,)), ((), ())), preferred_element_type=F32)
        parts = []
        for a in range(2):
            first = (a * NZ + zb) * (R * NC)
            cells = []
            for c in range(NC):
                teacher = pt[pl.ds(first + c, R, stride=NC), :]
                s = score[a * R:(a + 1) * R, c * R:(c + 1) * R]
                cells.append((jnp.tanh(s * half_scale + half_bias) - teacher).astype(BF))
            parts.append(jnp.concatenate(cells, axis=1))
        weight = jnp.concatenate(parts, axis=0)
        dI[zb] = jnp.dot(weight, texts, preferred_element_type=F32).reshape(2, R, E)
        dT[...] += lax.dot_general(
            weight, rows, (((0,), (0,)), ((), ())), preferred_element_type=F32
        ).reshape(NC, R, E)

    def i_send(sign, n):
        table = PLUS if sign == 1 else MINUS
        base = 0 if sign == 1 else 7
        dist, other, dep = table[n]
        a = l if sign == 1 else 1 - l
        col = 1 - a if other else a
        value = dI[zz(sign * dist), col]
        if dep is not None:
            i_copy(sign, dep).wait_recv()
            value = value + jr[base + dep].astype(F32)
        js[base + n] = value.astype(BF)
        i_copy(sign, n).start()

    def i_copy(sign, n):
        i = n if sign == 1 else 7 + n
        return remote(js.at[i], jr.at[i], isend.at[i], irecv.at[i], up if sign == 1 else down)

    order = (0, 1, -1, 2, 4, 3, -3, -2)

    def step(s, carry):
        @pl.when(s == 0)
        def _():
            for i in (2, 9):
                j_recv(i)
                j_copy(i + 2).start()

        @pl.when(s == 1)
        def _():
            for i in (3, 10):
                j_recv(i)
                j_copy(i + 2).start()

        @pl.when(s == 2)
        def _():
            j_recv(4)
            j_copy(6).start()
            j_recv(11)

        @pl.when(s == 3)
        def _():
            j_recv(12)
            j_copy(13).start()
            j_recv(5)

        @pl.when(s == 4)
        def _():
            j_recv(6)
            j_recv(13)

        @pl.when(s == 5)
        def _():
            i_send(1, 0)
            i_send(-1, 0)

        @pl.when(s == 6)
        def _():
            i_send(1, 1)
            i_send(1, 2)

        @pl.when(s == 7)
        def _():
            i_send(-1, 1)
            i_send(-1, 2)

        zb = jnp.int32(0)
        for n, d in enumerate(order):
            zb = jnp.where(s == n, zz(d), zb)
        pairs(zb)
        return carry

    lax.fori_loop(0, NZ, step, 0)

    spots = tuple((hh, dx) for dx in (2, 1, -1, 0) for hh in (0, 1))

    def d_copy(i):
        return remote(ds_.at[i], dr.at[i], dsend.at[i], drecv.at[i], core)

    def hcol(hh):
        return 1 - h if hh else h

    for i, (hh, dx) in enumerate(spots):
        ds_[i] = dT[blk(hcol(hh), x + dx, 1 - k)].astype(BF)
        d_copy(i).start()

    i_send(1, 3)
    i_send(-1, 3)

    def chip_sum(hh, dx):
        i = spots.index((hh, dx))
        d_copy(i).wait_recv()
        return dT[blk(hcol(hh), x + dx, k)] + dr[i].astype(F32)

    def x_copy(i):
        return remote(xs.at[i], xr.at[i], xsend.at[i], xrecv.at[i], right if i < 3 else left)

    def x_send(i, value):
        xs[i] = value.astype(BF)
        x_copy(i).start()

    def x_recv(i):
        x_copy(i).wait_recv()
        return xr[i].astype(F32)

    x_send(0, chip_sum(0, 2))
    x_send(3, chip_sum(1, 2))
    x_send(1, chip_sum(1, 1))
    x_send(4, chip_sum(0, -1))
    i_send(1, 4)
    i_send(-1, 4)
    x_send(2, chip_sum(0, 1) + x_recv(0))
    x_send(5, chip_sum(1, -1) + x_recv(3))
    i_send(1, 5)
    i_send(-1, 5)
    i_send(1, 6)
    i_send(-1, 6)

    def f_copy(i):
        return remote(fs.at[i], fr.at[i], fsend.at[i], frecv.at[i], yhi if i else ylo)

    fs[1] = (chip_sum(1, 0) + x_recv(1) + x_recv(5)).astype(BF)
    f_copy(1).start()
    own_text = chip_sum(0, 0) + x_recv(2) + x_recv(4)

    def i_recv(sign, n):
        i_copy(sign, n).wait_recv()
        return jr[n if sign == 1 else 7 + n].astype(F32)

    fs[0] = (dI[z, 1 - l] + i_recv(1, 5) + i_recv(-1, 5)).astype(BF)
    f_copy(0).start()

    f_copy(1).wait_recv()
    unit, mag = unit_rows(txt_ref[...].astype(F32))
    dtxt_ref[...] = unit_grad(half_scale * (own_text + fr[1].astype(F32)), unit, mag)

    own_image = dI[z, l] + i_recv(1, 6) + i_recv(-1, 6)
    f_copy(0).wait_recv()
    unit, mag = unit_rows(img_ref[...].astype(F32))
    dimg_ref[...] = unit_grad(half_scale * (own_image + fr[0].astype(F32)), unit, mag)

    for i in range(15):
        j_copy(i).wait_send()
        t_copy(i).wait_send()
    for n in range(7):
        i_copy(1, n).wait_send()
        i_copy(-1, n).wait_send()
    for i in range(8):
        d_copy(i).wait_send()
    for i in range(6):
        x_copy(i).wait_send()
    for i in range(2):
        f_copy(i).wait_send()


def shards(images, texts, teacher_codes, teacher_scales, student_logit_scale, logit_bias):
    vmem = pl.BlockSpec(memory_space=pltpu.VMEM)
    smem = pl.BlockSpec(memory_space=pltpu.SMEM)
    row = lambda *n: pltpu.VMEM((*n, R, E), BF)
    dma = lambda n: pltpu.SemaphoreType.DMA((n,))
    return pl.pallas_call(
        kernel,
        out_shape=(jax.ShapeDtypeStruct((R, E), F32), jax.ShapeDtypeStruct((R, E), F32)),
        in_specs=[vmem, vmem, pl.BlockSpec(memory_space=pl.ANY), vmem, smem, smem],
        out_specs=(vmem, vmem),
        scratch_shapes=[
            pltpu.VMEM((NC * R, NC, R), BF),
            pltpu.VMEM((NC, NC, R), F32),
            pltpu.VMEM((NC * R * NC, R), F32),
            row(NZ, 2),
            row(NC),
            pltpu.VMEM((NZ, 2, R, E), F32),
            pltpu.VMEM((NC, R, E), F32),
            row(14), row(14), row(8), row(8), row(6), row(6), row(2), row(2),
            dma(NC), dma(15), dma(15), dma(15), dma(15), dma(14), dma(14),
            dma(8), dma(8), dma(6), dma(6), dma(2), dma(2),
        ],
        compiler_params=pltpu.CompilerParams(
            collective_id=0, has_side_effects=True, vmem_limit_bytes=60 * 1024 * 1024
        ),
    )(images, texts, teacher_codes, jnp.swapaxes(teacher_scales, 1, 2), student_logit_scale, logit_bias)


def solution(mesh):
    in_specs = (
        P(("blk", "tile"), None),
        P(("blk", "tile"), None),
        P("blk", None, "tile"),
        P("blk", None, "tile"),
        P(),
        P(),
    )
    out_specs = (P(("blk", "tile"), None), P(("blk", "tile"), None))
    return jax.shard_map(shards, mesh=mesh, in_specs=in_specs, out_specs=out_specs, check_vma=False)
```

time: 400 us -> 79.3 us (0.20)
  waiting for transfers between devices: 233 us -> 0 us
  matrix products: 96 us -> 0 us
  Pallas kernels: 0 us -> 73.3 us
  starting transfers between devices: 25.4 us -> 0 us
  local copies, waits for them, and re-layouts: 22 us -> 3.34 us
  between operations: 15.4 us -> 1.93 us
  other arithmetic: 6.84 us -> 0 us
    dot_general x48 -> x0, matrix products: 96 us -> none  [the longest x16 53.8 us: pair_step(): lax.dot_general(every_img, text_rows, (((1,), (1,)), ((), ())), preferred...]
    ppermute x31 -> x0, waiting for transfers between devices: 91.5 us -> none  [from_behind(): return lax.ppermute(block, axis, route)]
    reduce_scatter x1 -> x0, waiting for transfers between devices: 77.1 us -> none  [shards(): lax.psum_scatter(gradient_picture, 'tile', scatter_dimension=0, tiled=True)]
    pallas_call x0 -> x1, Pallas kernels: none -> 73.3 us  [shards(): pl.pallas_call(kernel, out_shape=(jax.ShapeDtypeStruct((R, E), F32), jax....]
    all_gather x1 -> x0, waiting for transfers between devices: 64.1 us -> none  [shards(): lax.all_gather(image_unit.astype(jnp.bfloat16), 'tile', axis=0, tiled=True)]
    ppermute x31 -> x0, starting transfers between devices: 25.3 us -> none  [from_behind(): return lax.ppermute(block, axis, route)]
    while x76 -> x0, local copies, waits for them, and re-layouts: 11.7 us -> none
    unnamed x9 -> x2, local copies, waits for them, and re-layouts: 8.82 us -> 3.34 us
  transfers between devices with their start and end apart: 33 -> 0, of which waited for: 18 -> 0; matrix products, arithmetic and copies ran while one was open for 21% -> 0% of each run, Pallas kernels for 0% -> 0%
where the time goes in v1:
time: 79.3 us; the launch traced here: 78.6 us
  Pallas kernels  73.3 us (92%)
  local copies, waits for them, and re-layouts  3.34 us (4%)
  between operations  1.93 us (2%)
    pallas_call x1, Pallas kernels, shards(): pl.pallas_call(kernel, out_shape=(jax.ShapeDtypeStruct((R, E), F32), jax....  73.3 us
    unnamed x2, local copies, waits for them, and re-layouts  3.34 us

profile of v1, /device:TPU:2, one launch (start us, length us, event | category | flops | bytes accessed | tf_op | source)
XLA Modules:
  0.0 78.6 jit_solution(13310619359562198604)
XLA Ops:
  1.9 73.3 %shard_map.77 = (f32[128,512]{1,0:T(8,128)}, f32[128,512]{1,0:T(8,128)}) custom-call(bf16[128,512]{1,0:T(8,128)(2,1)} %img_ref.1, bf16[128,512]{1,0:T(8,128)(2,1)} %txt_ref.1, bf16[2048,16,128]{2,1,0:T(8,128)(2,1)} %codes_ref.1, f32[16,1,16]{2,1,0:T(1,128)} %bitcast.1, f32[1]{0:T(128)S(6)} %copy.10.scale_ref, f32[1]{0:T(128)S(6)} %copy.11.bias_ref), custom_call_target="tpu_custom_call" | custom-call | tf_op jit(solution)/shard_map/pallas_call | solution.py:343
  75.3 1.7 %copy.12 = f32[128,512]{1,0:T(8,128)} copy(f32[128,512]{1,0:T(8,128)} %get-tuple-element.4) | data formatting | bytes 524288
  77.0 1.7 %copy.13 = f32[128,512]{1,0:T(8,128)} copy(f32[128,512]{1,0:T(8,128)} %get-tuple-element.5) | data formatting | bytes 524288

commit v2 on v0

v2 whole, which is shorter than its diff:
```python
import jax
import jax.numpy as jnp
from jax import lax
from jax.experimental import pallas as pl
from jax.experimental.pallas import tpu as pltpu
from jax.sharding import PartitionSpec as P

EPS = 1e-06
F32 = jnp.float32
BF = jnp.bfloat16
R = 128
E = 512
NZ = 8
NX = 4
NC = 16
NH = 8
EARLY = 8
PIECES = {"": (0, R), "a": (0, R // 2), "b": (R // 2, R // 2)}

SCHEDULE = (
    "m0b", "xp0", "p0a", "yh", "xm0", "y0", "p0b", "c0", "m0a", "m1b", "p1a", "T", "m1a", "xp2a", "xm2b", "T",
    "T", "p1b", "c2", "xp1", "xm1", "m3b", "c4", "p3a", "T", "T", "y1", "c1", "m2", "p2", "T", "c3", "T", "T",
    "p3b", "y2", "m3a", "m4b", "p4a", "xp3a", "xm3b", "c6", "c5", (0, 0), "m5", (0, 2), (0, -1), "c7", (0, 1),
    (1, 1), "y3", "p5", (1, 2), "q4", (1, -1), (0, 3), (1, 3), "r4", "q5", (0, 4), (1, 4), "k2a", (1, -3),
    "k2b", (0, -3), "r5", (1, 0), (1, -2), "q0a", "k0a", "d7", "r0b", "d6", "k0b", "q1b", "r1a", "u10a",
    "v10b", (0, -2), "k1a", "u11b", "d5", "q1a", "d3", "r1b", "k1b", "v11a", "q2b", "u11a", "k3", "v11b",
    "u00a", "r2a", "d1", "d4", "d2", "v00b", "q2a", "r2b", "fa", "u01b", "q3b", "v01a", "r3a", "fb", "u01a",
    "v01b", "q3a", "r3b", "d0",
)
NEEDS = {
    "p1a": ("p0a",), "p1b": ("p0b",), "m1a": ("m0a",), "m1b": ("m0b",), "p2": ("y0",), "m2": ("y0",),
    "p3a": ("p1a",), "p3b": ("p1b",), "m3a": ("m1a",), "m3b": ("m1b",), "p4a": ("p3a",), "m4b": ("m3b",),
    "y1": ("m1a", "m1b"), "y2": ("p1a", "p1b"), "p5": ("y2",), "m5": ("y1",), "y3": ("p4a", "m4b"),
    "xp2a": ("xp0",), "xm2b": ("xm0",), "c1": ("xp0",), "c2": ("xm0",), "c3": ("xp2a", "xm2b"),
    "c4": ("yh",), "xp1": ("yh",), "xm1": ("yh",), "c5": ("xp1",), "c6": ("xm1",),
    "xp3a": ("xp1",), "xm3b": ("xm1",), "c7": ("xp3a", "xm3b"),
    "k3": ("q4", "r4"), "q0a": ("k2a",), "r0b": ("k2b",), "q1a": ("q0a",), "r1b": ("r0b",),
    "k0a": ("q5",), "k0b": ("q5",), "k1a": ("r5",), "k1b": ("r5",),
    "q2a": ("k0a", "q1a"), "q2b": ("k0b", "q1b"), "r2a": ("k1a", "r1a"), "r2b": ("k1b", "r1b"),
    "q3a": ("q2a",), "q3b": ("q2b",), "r3a": ("r2a",), "r3b": ("r2b",),
    "u10a": ("d7",), "v10b": ("d7",), "u11a": ("d6", "u10a"), "u11b": ("d6",),
    "v11a": ("d5",), "v11b": ("d5", "v10b"), "fa": ("d4", "u11a", "v11a"), "fb": ("d4", "u11b", "v11b"),
    "u00a": ("d3",), "v00b": ("d3",), "u01a": ("d2", "u00a"), "u01b": ("d2",),
    "v01a": ("d1",), "v01b": ("d1", "v00b"),
}
IMAGES = {
    0: ("y0",), 1: ("m0a", "m0b", "m2"), -1: ("p0a", "p0b", "p2"), 2: ("m1a", "m1b", "y1"),
    -2: ("p1a", "p1b", "y2"), 3: ("m3a", "m3b", "m5"), -3: ("p3a", "p3b", "p5"), 4: ("p4a", "m4b", "y3"),
}
TEXTS = (
    ("c0", "c1", "c2", "c3", "xp0", "xm0", "xp2a", "xm2b"),
    ("yh", "xp1", "xm1", "xp3a", "xm3b", "c4", "c5", "c6", "c7"),
)
LAST_TEXT = ("d0", "u01a", "u01b", "v01a", "v01b", "fa", "fb")
LAST_IMAGE = ("k3", "q3a", "q3b", "r3a", "r3b")
SUMS = {
    "q0": (4, 0), "q1": (3, 0), "q2": (2, 0), "q3": (1, 0), "q4": (1, 1), "q5": (3, 1),
    "r0": (4, 0), "r1": (-3, 0), "r2": (-2, 0), "r3": (-1, 0), "r4": (-1, 1), "r5": (-3, 1),
    "k0": (2, 1), "k1": (-2, 1), "k2": (4, 1), "k3": (0, 1),
}
SPOTS = ((0, 0), (0, -1), (0, 1), (0, 2), (1, 0), (1, -1), (1, 1), (1, 2))
X_SPOTS = {"u0": 3, "v0": 3, "u1": 2, "v1": 1}
COPIES = tuple(n for n in SCHEDULE if isinstance(n, str) and n != "T")
TILES = tuple(n for n in SCHEDULE if not isinstance(n, str))


def split(name):
    piece = name[-1] if name[-1] in "ab" else ""
    return name[: len(name) - len(piece)], pl.ds(*PIECES[piece])


def unit_rows(values):
    magnitude = jnp.sqrt(jnp.sum(values * values, axis=-1, keepdims=True) + EPS)
    return values / magnitude, magnitude


def unit_grad(grad_unit, unit_vectors, magnitude):
    inner = jnp.sum(unit_vectors * grad_unit, axis=-1, keepdims=True)
    return (grad_unit - unit_vectors * inner) / magnitude


def kernel(
    img_ref, txt_ref, codes_ref, scales_ref, scale_ref, bias_ref,
    dimg_ref, dtxt_ref,
    codes, scb, pt, J, T, dI, dT, zs, zr, ks, kr, ds_, dr, xs, xr, fs, fr,
    codes_sem, ssem, rsem,
):
    bi, ti = lax.axis_index("blk"), lax.axis_index("tile")
    h, x, k = bi // 8, (bi // 2) % NX, bi % 2
    l, z = ti // NZ, ti % NZ

    def blk(hh, xx, kk):
        return hh * 8 + ((xx + 8) % NX) * 2 + kk

    def zz(d):
        return (z + d + 16) % NZ

    def hcol(other):
        return 1 - h if other else h

    def lcol(other):
        return 1 - l if other else l

    up, down = {"tile": l * NZ + zz(1)}, {"tile": l * NZ + zz(-1)}
    ylo = {"tile": (1 - l) * NZ + z}
    yhi = {"blk": blk(1 - h, x, k)}
    right, left = {"blk": blk(h, x + 1, k)}, {"blk": blk(h, x - 1, k)}
    core = {"blk": blk(h, x, 1 - k)}

    def codes_copy(r):
        rows = pl.ds(r * R, R)
        return pltpu.make_async_copy(codes_ref.at[rows], codes.at[rows], codes_sem.at[r])

    barrier = pltpu.get_barrier_semaphore()
    for dev in (up, down, ylo, yhi, right, left, core):
        pl.semaphore_signal(barrier, inc=1, device_id=dev, device_id_type=pl.DeviceIdType.MESH)
    for r in range(NC):
        codes_copy(r).start()

    def landing(name):
        base, rows = split(name)
        i = int(base[1]) if base[0] in "qrkdu" or base[0] == "v" else 0
        if base[0] in "qr":
            return zs, zr, i if base[0] == "q" else 6 + i, rows
        if base[0] == "k":
            return ks, kr, i, rows
        if base[0] == "d":
            return ds_, dr, i, rows
        if base[0] == "f":
            return fs, fr, 0, rows
        return xs, xr, i * 4 + int(base[2]) * 2 + (base[0] == "v"), rows

    def copy(name):
        base, rows = split(name)
        kind = base[0]
        if kind in "pmy" and base != "yh":
            n = int(base[1])
            dz = {"p": (0, -1, 0, -2, -3, -2), "m": (0, 1, 0, 2, 3, 2), "y": (0, 2, -2, 4)}[kind][n]
            spot = J.at[zz(dz), lcol(kind != "y" and n in (2, 5)), rows]
            src, dst, dev = spot, spot, {"p": up, "m": down, "y": ylo}[kind]
        elif kind in "xyc":
            if base == "yh":
                spot, dev = T.at[bi, rows], yhi
            elif kind == "c":
                hh, dx = SPOTS[int(base[1])]
                spot, dev = T.at[blk(hcol(hh), x + dx, k), rows], core
            else:
                n, sign = int(base[2]), 1 if base[1] == "p" else -1
                spot = T.at[blk(hcol(n % 2), x - sign if n >= 2 else x, k), rows]
                dev = right if sign == 1 else left
            src, dst = spot, spot
        else:
            out, into, i, rows = landing(name)
            src, dst = out.at[i, rows], into.at[i, rows]
            dev = {"q": up, "r": down, "k": ylo, "d": core, "u": right, "v": left, "f": yhi}[kind]
        i = COPIES.index(name)
        return pltpu.make_async_remote_copy(
            src_ref=src, dst_ref=dst, send_sem=ssem.at[i], recv_sem=rsem.at[i], device_id=dev,
            device_id_type=pl.DeviceIdType.MESH,
        )

    seen = set()

    def arrive(names):
        for name in names:
            if name not in seen:
                seen.add(name)
                copy(name).wait_recv()

    img_unit, _ = unit_rows(img_ref[...].astype(F32))
    J[z, l] = img_unit.astype(BF)
    txt_unit, _ = unit_rows(txt_ref[...].astype(F32))
    T[bi] = txt_unit.astype(BF)

    eye = lax.broadcasted_iota(jnp.int32, (NC, NC), 0) == lax.broadcasted_iota(jnp.int32, (NC, NC), 1)
    for r in range(NC):
        row = jnp.broadcast_to(scales_ref[r], (NC, NC))
        column = jnp.sum(jnp.where(eye, row, 0.0), axis=-1, keepdims=True)
        scb[r] = jnp.broadcast_to(0.5 * column, (NC, R))

    def teacher_rows(r, carry):
        codes_copy(r).wait()
        sc = scb[r]
        dT[r] = jnp.zeros((R, E), F32)
        dI[r // 2, r % 2] = jnp.zeros((R, E), F32)

        def some(g, inner):
            for u in range(16):
                i = r * R + g * 16 + u
                pt[pl.ds(pl.multiple_of(i * NC, NC), NC), :] = jnp.tanh(codes[i].astype(F32) * sc)
            return inner

        return lax.fori_loop(0, R // 16, some, carry)

    half_scale = 0.5 * scale_ref[0]
    half_bias = 0.5 * bias_ref[0]

    def pairs(zb, hb):
        rows = J[zb].reshape(2 * R, E)
        columns = pl.ds(hb * NH, NH)
        texts = T[columns].reshape(NH * R, E)
        score = lax.dot_general(rows, texts, (((1,), (1,)), ((), ())), preferred_element_type=F32)
        parts = []
        for a in range(2):
            first = (a * NZ + zb) * (R * NC) + hb * NH
            cells = []
            for c in range(NH):
                teacher = pt[pl.ds(first + c, R, stride=NC), :]
                s = score[a * R:(a + 1) * R, c * R:(c + 1) * R]
                cells.append((jnp.tanh(s * half_scale + half_bias) - teacher).astype(BF))
            parts.append(jnp.concatenate(cells, axis=1))
        weight = jnp.concatenate(parts, axis=0)
        dI[zb] += jnp.dot(weight, texts, preferred_element_type=F32).reshape(2, R, E)
        dT[columns] += lax.dot_general(
            weight, rows, (((0,), (0,)), ((), ())), preferred_element_type=F32
        ).reshape(NH, R, E)

    def chip_sum(i, rows):
        hh, dx = SPOTS[i]
        return dT[blk(hcol(hh), x + dx, k), rows] + dr[i, rows].astype(F32)

    def arrived(name, rows):
        _, into, i, _ = landing(name)
        return into[i, rows].astype(F32)

    def send(name):
        needs = NEEDS.get(name, ())
        arrive(needs)
        base, rows = split(name)
        kind = base[0]
        value = None
        if kind in "qrk":
            dz, other = SUMS[base]
            value = dI[zz(dz), lcol(other), rows]
        elif kind == "d":
            hh, dx = SPOTS[int(base[1])]
            value = dT[blk(hcol(hh), x + dx, 1 - k), rows]
        elif kind in "uv":
            value = chip_sum(4 * int(base[1]) + X_SPOTS[kind + base[2]], rows)
        elif kind == "f":
            value = chip_sum(4, rows)
        if value is not None:
            for other in needs:
                if other[0] != "d":
                    value = value + arrived(other, rows)
            out, _, i, _ = landing(name)
            out[i, rows] = value.astype(BF)
        copy(name).start()

    before, events = [], {0: []}
    for item in SCHEDULE:
        if not isinstance(item, str):
            events[len(events)] = []
        elif len(events) == 1:
            before.append(item)
        else:
            events[len(events) - 1].append(item)

    lax.fori_loop(0, EARLY, teacher_rows, 0)
    pl.semaphore_wait(barrier, 7)
    done = EARLY
    for n, name in enumerate(before):
        if name != "T":
            send(name)
        elif n + 1 == len(before) or before[n + 1] != "T":
            first, run = done, 1
            while run <= n and before[n - run] == "T":
                run += 1
            done = first + run
            lax.fori_loop(first, done, teacher_rows, 0)

    def step(s, carry):
        for n, (hh, d) in enumerate(TILES):
            names = events[n] if n else ()
            waits = tuple(w for w in IMAGES[d] + TEXTS[hh] if w not in seen)
            if names or waits:

                def event(names=names, waits=waits):
                    for name in names:
                        send(name)
                    arrive(waits)

                pl.when(s == n)(event)
        zb, hb = jnp.int32(0), jnp.int32(0)
        for n, (hh, d) in enumerate(TILES):
            zb = jnp.where(s == n, zz(d), zb)
            hb = jnp.where(s == n, hcol(hh), hb)
        pairs(zb, hb)
        return carry

    lax.fori_loop(0, len(TILES), step, 0)
    for name in events[len(TILES)]:
        send(name)

    whole = pl.ds(0, R)
    unit, mag = unit_rows(txt_ref[...].astype(F32))
    arrive(LAST_TEXT)
    grad = chip_sum(0, whole) + arrived("u01", whole) + arrived("v01", whole) + arrived("f", whole)
    dtxt_ref[...] = unit_grad(half_scale * grad, unit, mag)

    unit, mag = unit_rows(img_ref[...].astype(F32))
    arrive(LAST_IMAGE)
    grad = dI[z, l] + arrived("k3", whole) + arrived("q3", whole) + arrived("r3", whole)
    dimg_ref[...] = unit_grad(half_scale * grad, unit, mag)

    for name in COPIES:
        copy(name).wait_send()


def hand_out(a_ref, b_ref, a_out, b_out):
    a_out[...] = a_ref[...]
    b_out[...] = b_ref[...]


def shards(images, texts, teacher_codes, teacher_scales, student_logit_scale, logit_bias):
    vmem = pl.BlockSpec(memory_space=pltpu.VMEM)
    smem = pl.BlockSpec(memory_space=pltpu.SMEM)
    row = lambda *n: pltpu.VMEM((*n, R, E), BF)
    dma = lambda n: pltpu.SemaphoreType.DMA((n,))
    out = jax.ShapeDtypeStruct((R, E), F32)
    grads = pl.pallas_call(
        kernel,
        out_shape=(out, out),
        in_specs=[vmem, vmem, pl.BlockSpec(memory_space=pl.ANY), vmem, smem, smem],
        out_specs=(vmem, vmem),
        scratch_shapes=[
            pltpu.VMEM((NC * R, NC, R), BF),
            pltpu.VMEM((NC, NC, R), F32),
            pltpu.VMEM((NC * R * NC, R), F32),
            row(NZ, 2),
            row(NC),
            pltpu.VMEM((NZ, 2, R, E), F32),
            pltpu.VMEM((NC, R, E), F32),
            row(12), row(12), row(4), row(4), row(8), row(8), row(8), row(8), row(1), row(1),
            dma(NC), dma(len(COPIES)), dma(len(COPIES)),
        ],
        compiler_params=pltpu.CompilerParams(
            collective_id=0, has_side_effects=True, vmem_limit_bytes=54 * 1024 * 1024
        ),
    )(images, texts, teacher_codes, jnp.swapaxes(teacher_scales, 1, 2), student_logit_scale, logit_bias)
    return pl.pallas_call(hand_out, out_shape=(out, out), in_specs=[vmem] * 2, out_specs=(vmem,) * 2)(*grads)


def solution(mesh):
    in_specs = (
        P(("blk", "tile"), None),
        P(("blk", "tile"), None),
        P("blk", None, "tile"),
        P("blk", None, "tile"),
        P(),
        P(),
    )
    out_specs = (P(("blk", "tile"), None), P(("blk", "tile"), None))
    return jax.shard_map(shards, mesh=mesh, in_specs=in_specs, out_specs=out_specs, check_vma=False)
```

time: 400 us -> 64.8 us (0.16)
  waiting for transfers between devices: 233 us -> 0 us
  matrix products: 96 us -> 0 us
  Pallas kernels: 0 us -> 62.5 us
  starting transfers between devices: 25.4 us -> 0 us
  local copies, waits for them, and re-layouts: 22 us -> 0 us
  between operations: 15.4 us -> 1.93 us
  other arithmetic: 6.84 us -> 0 us
    dot_general x48 -> x0, matrix products: 96 us -> none  [the longest x16 53.8 us: pair_step(): lax.dot_general(every_img, text_rows, (((1,), (1,)), ((), ())), preferred...]
    ppermute x31 -> x0, waiting for transfers between devices: 91.5 us -> none  [from_behind(): return lax.ppermute(block, axis, route)]
    reduce_scatter x1 -> x0, waiting for transfers between devices: 77.1 us -> none  [shards(): lax.psum_scatter(gradient_picture, 'tile', scatter_dimension=0, tiled=True)]
    all_gather x1 -> x0, waiting for transfers between devices: 64.1 us -> none  [shards(): lax.all_gather(image_unit.astype(jnp.bfloat16), 'tile', axis=0, tiled=True)]
    pallas_call x0 -> x2, Pallas kernels: none -> 62.5 us  [the longest x1 60.7 us: shards(): pl.pallas_call(kernel, out_shape=(out, out), in_specs=[vmem, vmem, pl.Blo...]
    ppermute x31 -> x0, starting transfers between devices: 25.3 us -> none  [from_behind(): return lax.ppermute(block, axis, route)]
    while x76 -> x0, local copies, waits for them, and re-layouts: 11.7 us -> none
    unnamed x9 -> x0, local copies, waits for them, and re-layouts: 8.82 us -> none
  transfers between devices with their start and end apart: 33 -> 0, of which waited for: 18 -> 0; matrix products, arithmetic and copies ran while one was open for 21% -> 0% of each run, Pallas kernels for 0% -> 0%
where the time goes in v2:
time: 64.8 us; the launch traced here: 64.5 us
  Pallas kernels  62.5 us (96%)
  between operations  1.93 us (3%)
    pallas_call x1, Pallas kernels, shards(): pl.pallas_call(kernel, out_shape=(out, out), in_specs=[vmem, vmem, pl.Blo...  60.7 us
    pallas_call x1, Pallas kernels, shards(): pl.pallas_call(hand_out, out_shape=(out, out), in_specs=[vmem] * 2, out_s...  1.84 us

profile of v2, /device:TPU:2, one launch (start us, length us, event | category | flops | bytes accessed | tf_op | source)
XLA Modules:
  0.0 64.5 jit_solution(12851069492204648608)
XLA Ops:
  1.9 60.7 %shard_map.77 = (f32[128,512]{1,0:T(8,128)}, f32[128,512]{1,0:T(8,128)}) custom-call(bf16[128,512]{1,0:T(8,128)(2,1)} %img_ref.1, bf16[128,512]{1,0:T(8,128)(2,1)} %txt_ref.1, bf16[2048,16,128]{2,1,0:T(8,128)(2,1)} %codes_ref.1, f32[16,1,16]{2,1,0:T(1,128)} %bitcast.1, f32[1]{0:T(128)S(6)} %copy.8.scale_ref, f32[1]{0:T(128)S(6)} %copy.9.bias_ref), custom_call_target="tpu_custom_call" | custom-call | tf_op jit(solution)/shard_map/pallas_call | solution.py:321
  62.6 1.8 %shard_map.78 = (f32[128,512]{1,0:T(8,128)}, f32[128,512]{1,0:T(8,128)}) custom-call(f32[128,512]{1,0:T(8,128)} %get-tuple-element.4.a_ref, f32[128,512]{1,0:T(8,128)} %get-tuple-element.5.b_ref), custom_call_target="tpu_custom_call" | custom-call | tf_op jit(solution)/shard_map/pallas_call | solution.py:341

commit v3 on v2

--- a/solution.py
+++ b/solution.py
@@ -14,34 +14,32 @@
 NX = 4
 NC = 16
 NH = 8
+PITCH = NC * R + 8
 EARLY = 8
 PIECES = {"": (0, R), "a": (0, R // 2), "b": (R // 2, R // 2)}
 
 SCHEDULE = (
-    "m0b", "xp0", "p0a", "yh", "xm0", "y0", "p0b", "c0", "m0a", "m1b", "p1a", "T", "m1a", "xp2a", "xm2b", "T",
-    "T", "p1b", "c2", "xp1", "xm1", "m3b", "c4", "p3a", "T", "T", "y1", "c1", "m2", "p2", "T", "c3", "T", "T",
-    "p3b", "y2", "m3a", "m4b", "p4a", "xp3a", "xm3b", "c6", "c5", (0, 0), "m5", (0, 2), (0, -1), "c7", (0, 1),
-    (1, 1), "y3", "p5", (1, 2), "q4", (1, -1), (0, 3), (1, 3), "r4", "q5", (0, 4), (1, 4), "k2a", (1, -3),
-    "k2b", (0, -3), "r5", (1, 0), (1, -2), "q0a", "k0a", "d7", "r0b", "d6", "k0b", "q1b", "r1a", "u10a",
-    "v10b", (0, -2), "k1a", "u11b", "d5", "q1a", "d3", "r1b", "k1b", "v11a", "q2b", "u11a", "k3", "v11b",
-    "u00a", "r2a", "d1", "d4", "d2", "v00b", "q2a", "r2b", "fa", "u01b", "q3b", "v01a", "r3a", "fb", "u01a",
-    "v01b", "q3a", "r3b", "d0",
+    "yh", "p0a", "m0b", "xm0", "xp0", "m0a", "p0b", "T", "p1a", "y0", "m1b", "p1b", "m1a", "xp1", "xm1", "T",
+    "xm2b", "p3a", "m3b", "xp2a", "c0", "T", "c2", "p2", "y2", "m2", "xp3a", "xm3b", "T", "c5", "p4a", "T",
+    "c6", "m4b", "m3a", "p3b", "y1", "c3", "T", "c1", "T", "c4", "p5", "T", "c7", (0, -1), "y3", (1, -1),
+    (1, 0), "m5", (2, 1), "q4", (2, -3), "r5", (2, 4), "k2b", "k2a", (2, 3), "q5", "r4", (2, -2), "k1a", "r0b",
+    (1, 2), "q0a", "r1a", "d7", "k1b", "d6", "d5", (0, 2), "u10a", "v10b", "k0b", "q1b", (0, 0), "d4", "u11b",
+    "k0a", "d2", "r1b", "q1a", "v11a", "d3", "k3", "d1", "u11a", "u00a", "r2a", "v11b", "q2b", "v00b", "r2b",
+    "q2a", "v01a", "fa", "u01b", "q3b", "u01a", "r3a", "v01b", "fb", "r3b", "d0", "q3a",
 )
 NEEDS = {
     "p1a": ("p0a",), "p1b": ("p0b",), "m1a": ("m0a",), "m1b": ("m0b",), "p2": ("y0",), "m2": ("y0",),
     "p3a": ("p1a",), "p3b": ("p1b",), "m3a": ("m1a",), "m3b": ("m1b",), "p4a": ("p3a",), "m4b": ("m3b",),
     "y1": ("m1a", "m1b"), "y2": ("p1a", "p1b"), "p5": ("y2",), "m5": ("y1",), "y3": ("p4a", "m4b"),
-    "xp2a": ("xp0",), "xm2b": ("xm0",), "c1": ("xp0",), "c2": ("xm0",), "c3": ("xp2a", "xm2b"),
-    "c4": ("yh",), "xp1": ("yh",), "xm1": ("yh",), "c5": ("xp1",), "c6": ("xm1",),
-    "xp3a": ("xp1",), "xm3b": ("xm1",), "c7": ("xp3a", "xm3b"),
-    "k3": ("q4", "r4"), "q0a": ("k2a",), "r0b": ("k2b",), "q1a": ("q0a",), "r1b": ("r0b",),
-    "k0a": ("q5",), "k0b": ("q5",), "k1a": ("r5",), "k1b": ("r5",),
-    "q2a": ("k0a", "q1a"), "q2b": ("k0b", "q1b"), "r2a": ("k1a", "r1a"), "r2b": ("k1b", "r1b"),
-    "q3a": ("q2a",), "q3b": ("q2b",), "r3a": ("r2a",), "r3b": ("r2b",),
-    "u10a": ("d7",), "v10b": ("d7",), "u11a": ("d6", "u10a"), "u11b": ("d6",),
-    "v11a": ("d5",), "v11b": ("d5", "v10b"), "fa": ("d4", "u11a", "v11a"), "fb": ("d4", "u11b", "v11b"),
-    "u00a": ("d3",), "v00b": ("d3",), "u01a": ("d2", "u00a"), "u01b": ("d2",),
-    "v01a": ("d1",), "v01b": ("d1", "v00b"),
+    "xp2a": ("xp0",), "xm2b": ("xm0",), "c1": ("xp0",), "c2": ("xm0",), "c3": ("xp2a", "xm2b"), "c4": ("yh",),
+    "xp1": ("yh",), "xm1": ("yh",), "c5": ("xp1",), "c6": ("xm1",), "xp3a": ("xp1",), "xm3b": ("xm1",),
+    "c7": ("xp3a", "xm3b"), "k3": ("q4", "r4"), "q0a": ("k2a",), "r0b": ("k2b",), "q1a": ("q0a",),
+    "r1b": ("r0b",), "k0a": ("q5",), "k0b": ("q5",), "k1a": ("r5",), "k1b": ("r5",), "q2a": ("k0a", "q1a"),
+    "q2b": ("k0b", "q1b"), "r2a": ("k1a", "r1a"), "r2b": ("k1b", "r1b"), "q3a": ("q2a",), "q3b": ("q2b",),
+    "r3a": ("r2a",), "r3b": ("r2b",), "u10a": ("d7",), "v10b": ("d7",), "u11b": ("d6",), "v11a": ("d5",),
+    "u11a": ("d6", "u10a"), "v11b": ("d5", "v10b"), "fa": ("d4", "u11a", "v11a"), "fb": ("d4", "u11b", "v11b"),
+    "u00a": ("d3",), "v00b": ("d3",), "u01b": ("d2",), "v01a": ("d1",), "u01a": ("d2", "u00a"),
+    "v01b": ("d1", "v00b"),
 }
 IMAGES = {
     0: ("y0",), 1: ("m0a", "m0b", "m2"), -1: ("p0a", "p0b", "p2"), 2: ("m1a", "m1b", "y1"),
@@ -56,10 +54,10 @@
 SUMS = {
     "q0": (4, 0), "q1": (3, 0), "q2": (2, 0), "q3": (1, 0), "q4": (1, 1), "q5": (3, 1),
     "r0": (4, 0), "r1": (-3, 0), "r2": (-2, 0), "r3": (-1, 0), "r4": (-1, 1), "r5": (-3, 1),
-    "k0": (2, 1), "k1": (-2, 1), "k2": (4, 1), "k3": (0, 1),
+    "g0": (4, 1), "g1": (4, 1), "k0": (2, 1), "k1": (-2, 1), "k2": (4, 1), "k3": (0, 1),
 }
 SPOTS = ((0, 0), (0, -1), (0, 1), (0, 2), (1, 0), (1, -1), (1, 1), (1, 2))
-X_SPOTS = {"u0": 3, "v0": 3, "u1": 2, "v1": 1}
+X_SPOTS = {"u0": 3, "v0": 3, "u1": 2, "v1": 1, "w": 3}
 COPIES = tuple(n for n in SCHEDULE if isinstance(n, str) and n != "T")
 TILES = tuple(n for n in SCHEDULE if not isinstance(n, str))
 
@@ -82,7 +80,7 @@
 def kernel(
     img_ref, txt_ref, codes_ref, scales_ref, scale_ref, bias_ref,
     dimg_ref, dtxt_ref,
-    codes, scb, pt, J, T, dI, dT, zs, zr, ks, kr, ds_, dr, xs, xr, fs, fr,
+    codes, scb, pt, J, T, dI, dT, zs, zr, ks, kr, ds_, dr, xs, xr, fs, fr, gs, gr, ws, wr,
     codes_sem, ssem, rsem,
 ):
     bi, ti = lax.axis_index("blk"), lax.axis_index("tile")
@@ -106,24 +104,35 @@
     yhi = {"blk": blk(1 - h, x, k)}
     right, left = {"blk": blk(h, x + 1, k)}, {"blk": blk(h, x - 1, k)}
     core = {"blk": blk(h, x, 1 - k)}
+    across = {"blk": blk(h, x + 2, k)}
+    up_ylo, down_ylo = {"tile": (1 - l) * NZ + zz(1)}, {"tile": (1 - l) * NZ + zz(-1)}
+    partners = [up, down, ylo, yhi, right, left, core]
+    if any(n[0] == "g" for n in COPIES):
+        partners += [up_ylo, down_ylo]
+    if any(n[0] == "w" or n[:2] == "xx" for n in COPIES):
+        partners += [across]
 
     def codes_copy(r):
         rows = pl.ds(r * R, R)
         return pltpu.make_async_copy(codes_ref.at[rows], codes.at[rows], codes_sem.at[r])
 
     barrier = pltpu.get_barrier_semaphore()
-    for dev in (up, down, ylo, yhi, right, left, core):
+    for dev in partners:
         pl.semaphore_signal(barrier, inc=1, device_id=dev, device_id_type=pl.DeviceIdType.MESH)
     for r in range(NC):
         codes_copy(r).start()
 
     def landing(name):
         base, rows = split(name)
-        i = int(base[1]) if base[0] in "qrkdu" or base[0] == "v" else 0
+        i = int(base[1]) if base[0] in "qrkgduvw" else 0
         if base[0] in "qr":
             return zs, zr, i if base[0] == "q" else 6 + i, rows
         if base[0] == "k":
             return ks, kr, i, rows
+        if base[0] == "g":
+            return gs, gr, i, rows
+        if base[0] == "w":
+            return ws, wr, i, rows
         if base[0] == "d":
             return ds_, dr, i, rows
         if base[0] == "f":
@@ -135,12 +144,16 @@
         kind = base[0]
         if kind in "pmy" and base != "yh":
             n = int(base[1])
-            dz = {"p": (0, -1, 0, -2, -3, -2), "m": (0, 1, 0, 2, 3, 2), "y": (0, 2, -2, 4)}[kind][n]
+            dz = {"p": (0, -1, 0, -2, -3, -2, -3), "m": (0, 1, 0, 2, 3, 2, 3), "y": (0, 2, -2, 4)}[kind][n]
             spot = J.at[zz(dz), lcol(kind != "y" and n in (2, 5)), rows]
             src, dst, dev = spot, spot, {"p": up, "m": down, "y": ylo}[kind]
+            if n == 6:
+                dev = up_ylo if kind == "p" else down_ylo
         elif kind in "xyc":
             if base == "yh":
                 spot, dev = T.at[bi, rows], yhi
+            elif base[:2] == "xx":
+                spot, dev = T.at[blk(hcol(base == "xx3"), x, k), rows], across
             elif kind == "c":
                 hh, dx = SPOTS[int(base[1])]
                 spot, dev = T.at[blk(hcol(hh), x + dx, k), rows], core
@@ -152,7 +165,7 @@
         else:
             out, into, i, rows = landing(name)
             src, dst = out.at[i, rows], into.at[i, rows]
-            dev = {"q": up, "r": down, "k": ylo, "d": core, "u": right, "v": left, "f": yhi}[kind]
+            dev = {"g": down_ylo if i else up_ylo, "w": across, "q": up, "r": down, "k": ylo, "d": core, "u": right, "v": left, "f": yhi}[kind]
         i = COPIES.index(name)
         return pltpu.make_async_remote_copy(
             src_ref=src, dst_ref=dst, send_sem=ssem.at[i], recv_sem=rsem.at[i], device_id=dev,
@@ -187,7 +200,7 @@
         def some(g, inner):
             for u in range(16):
                 i = r * R + g * 16 + u
-                pt[pl.ds(pl.multiple_of(i * NC, NC), NC), :] = jnp.tanh(codes[i].astype(F32) * sc)
+                pt[pl.ds(i, NC, stride=PITCH), :] = jnp.tanh(codes[i].astype(F32) * sc)
             return inner
 
         return lax.fori_loop(0, R // 16, some, carry)
@@ -195,25 +208,26 @@
     half_scale = 0.5 * scale_ref[0]
     half_bias = 0.5 * bias_ref[0]
 
-    def pairs(zb, hb):
+    def pairs(zb, hb, count):
         rows = J[zb].reshape(2 * R, E)
-        columns = pl.ds(hb * NH, NH)
-        texts = T[columns].reshape(NH * R, E)
+        columns = pl.ds(hb * NH, count)
+        texts = T[columns].reshape(count * R, E)
         score = lax.dot_general(rows, texts, (((1,), (1,)), ((), ())), preferred_element_type=F32)
         parts = []
         for a in range(2):
-            first = (a * NZ + zb) * (R * NC) + hb * NH
+            first = hb * (NH * PITCH) + (a * NZ + zb) * R
             cells = []
-            for c in range(NH):
-                teacher = pt[pl.ds(first + c, R, stride=NC), :]
+            for c in range(count):
+                teacher = pt[pl.ds(pl.multiple_of(first + c * PITCH, 8), R), :]
                 s = score[a * R:(a + 1) * R, c * R:(c + 1) * R]
                 cells.append((jnp.tanh(s * half_scale + half_bias) - teacher).astype(BF))
             parts.append(jnp.concatenate(cells, axis=1))
         weight = jnp.concatenate(parts, axis=0)
-        dI[zb] += jnp.dot(weight, texts, preferred_element_type=F32).reshape(2, R, E)
+        part = jnp.dot(weight, texts, preferred_element_type=F32).reshape(2, R, E)
+        dI[zb] = part if count == NC else dI[zb] + part
         dT[columns] += lax.dot_general(
             weight, rows, (((0,), (0,)), ((), ())), preferred_element_type=F32
-        ).reshape(NH, R, E)
+        ).reshape(count, R, E)
 
     def chip_sum(i, rows):
         hh, dx = SPOTS[i]
@@ -229,14 +243,14 @@
         base, rows = split(name)
         kind = base[0]
         value = None
-        if kind in "qrk":
+        if kind in "qrkg":
             dz, other = SUMS[base]
             value = dI[zz(dz), lcol(other), rows]
         elif kind == "d":
             hh, dx = SPOTS[int(base[1])]
             value = dT[blk(hcol(hh), x + dx, 1 - k), rows]
-        elif kind in "uv":
-            value = chip_sum(4 * int(base[1]) + X_SPOTS[kind + base[2]], rows)
+        elif kind in "uvw":
+            value = chip_sum(4 * int(base[1]) + X_SPOTS[kind + base[2:]], rows)
         elif kind == "f":
             value = chip_sum(4, rows)
         if value is not None:
@@ -257,7 +271,7 @@
             events[len(events) - 1].append(item)
 
     lax.fori_loop(0, EARLY, teacher_rows, 0)
-    pl.semaphore_wait(barrier, 7)
+    pl.semaphore_wait(barrier, len(partners))
     done = EARLY
     for n, name in enumerate(before):
         if name != "T":
@@ -272,7 +286,8 @@
     def step(s, carry):
         for n, (hh, d) in enumerate(TILES):
             names = events[n] if n else ()
-            waits = tuple(w for w in IMAGES[d] + TEXTS[hh] if w not in seen)
+            texts = TEXTS[hh] if hh < 2 else TEXTS[0] + TEXTS[1]
+            waits = tuple(w for w in IMAGES[d] + texts if w not in seen)
             if names or waits:
 
                 def event(names=names, waits=waits):
@@ -281,11 +296,15 @@
                     arrive(waits)
 
                 pl.when(s == n)(event)
-        zb, hb = jnp.int32(0), jnp.int32(0)
+        zb, hb, full = jnp.int32(0), jnp.int32(0), jnp.int32(0)
         for n, (hh, d) in enumerate(TILES):
             zb = jnp.where(s == n, zz(d), zb)
-            hb = jnp.where(s == n, hcol(hh), hb)
-        pairs(zb, hb)
+            if hh < 2:
+                hb = jnp.where(s == n, hcol(hh), hb)
+            else:
+                full = jnp.where(s == n, 1, full)
+        pl.when(full == 0)(lambda: pairs(zb, hb, NH))
+        pl.when(full == 1)(lambda: pairs(zb, 0, NC))
         return carry
 
     lax.fori_loop(0, len(TILES), step, 0)
@@ -295,7 +314,9 @@
     whole = pl.ds(0, R)
     unit, mag = unit_rows(txt_ref[...].astype(F32))
     arrive(LAST_TEXT)
-    grad = chip_sum(0, whole) + arrived("u01", whole) + arrived("v01", whole) + arrived("f", whole)
+    grad = chip_sum(0, whole)
+    for name in sorted({split(n)[0] for n in LAST_TEXT if n[0] != "d"}):
+        grad = grad + arrived(name, whole)
     dtxt_ref[...] = unit_grad(half_scale * grad, unit, mag)
 
     unit, mag = unit_rows(img_ref[...].astype(F32))
@@ -305,11 +326,6 @@
 
     for name in COPIES:
         copy(name).wait_send()
-
-
-def hand_out(a_ref, b_ref, a_out, b_out):
-    a_out[...] = a_ref[...]
-    b_out[...] = b_ref[...]
 
 
 def shards(images, texts, teacher_codes, teacher_scales, student_logit_scale, logit_bias):
@@ -317,8 +333,8 @@
     smem = pl.BlockSpec(memory_space=pltpu.SMEM)
     row = lambda *n: pltpu.VMEM((*n, R, E), BF)
     dma = lambda n: pltpu.SemaphoreType.DMA((n,))
-    out = jax.ShapeDtypeStruct((R, E), F32)
-    grads = pl.pallas_call(
+    out = pltpu.VMEM((R, E), F32)
+    return pl.pallas_call(
         kernel,
         out_shape=(out, out),
         in_specs=[vmem, vmem, pl.BlockSpec(memory_space=pl.ANY), vmem, smem, smem],
@@ -326,19 +342,18 @@
         scratch_shapes=[
             pltpu.VMEM((NC * R, NC, R), BF),
             pltpu.VMEM((NC, NC, R), F32),
-            pltpu.VMEM((NC * R * NC, R), F32),
+            pltpu.VMEM((NC * PITCH, R), F32),
             row(NZ, 2),
             row(NC),
             pltpu.VMEM((NZ, 2, R, E), F32),
             pltpu.VMEM((NC, R, E), F32),
-            row(12), row(12), row(4), row(4), row(8), row(8), row(8), row(8), row(1), row(1),
+            row(12), row(12), row(4), row(4), row(8), row(8), row(8), row(8), row(1), row(1), row(2), row(2), row(2), row(2),
             dma(NC), dma(len(COPIES)), dma(len(COPIES)),
         ],
         compiler_params=pltpu.CompilerParams(
             collective_id=0, has_side_effects=True, vmem_limit_bytes=54 * 1024 * 1024
         ),
     )(images, texts, teacher_codes, jnp.swapaxes(teacher_scales, 1, 2), student_logit_scale, logit_bias)
-    return pl.pallas_call(hand_out, out_shape=(out, out), in_specs=[vmem] * 2, out_specs=(vmem,) * 2)(*grads)
 
 
 def solution(mesh):

time: 64.8 us -> 60.3 us (0.931)
  Pallas kernels: 62.5 us -> 56.5 us
  local copies, waits for them, and re-layouts: 0 us -> 1.41 us
    pallas_call x1, Pallas kernels: 60.7 us -> 56.5 us  [shards(): pl.pallas_call(kernel, out_shape=(out, out), in_specs=[vmem, vmem, pl.Blo...]
    pallas_call x1 -> x0, Pallas kernels: 1.84 us -> none  [shards(): pl.pallas_call(hand_out, out_shape=(out, out), in_specs=[vmem] * 2, out_s...]
    unnamed x0 -> x2, local copies, waits for them, and re-layouts: none -> 1.41 us
where the time goes in v3:
time: 60.3 us; the launch traced here: 59.9 us
  Pallas kernels  56.5 us (94%)
  between operations  1.93 us (3%)
  local copies, waits for them, and re-layouts  1.41 us (2%)
    pallas_call x1, Pallas kernels, shards(): pl.pallas_call(kernel, out_shape=(out, out), in_specs=[vmem, vmem, pl.Blo...  56.5 us
    unnamed x2, local copies, waits for them, and re-layouts  1.41 us

profile of v3, /device:TPU:2, one launch (start us, length us, event | category | flops | bytes accessed | tf_op | source)
XLA Modules:
  0.0 59.9 jit_solution(10993608021851887958)
XLA Ops:
  1.9 56.5 %shard_map.77 = (f32[128,512]{1,0:T(8,128)S(1)}, f32[128,512]{1,0:T(8,128)S(1)}) custom-call(bf16[128,512]{1,0:T(8,128)(2,1)} %img_ref.1, bf16[128,512]{1,0:T(8,128)(2,1)} %txt_ref.1, bf16[2048,16,128]{2,1,0:T(8,128)(2,1)} %codes_ref.1, f32[16,1,16]{2,1,0:T(1,128)} %bitcast.1, f32[1]{0:T(128)S(6)} %copy.12.scale_ref, f32[1]{0:T(128)S(6)} %copy.13.bias_ref), custom_call_target="tpu_custom_call" | custom-call | tf_op jit(solution)/shard_map/pallas_call | solution.py:337
  58.5 0.7 %copy.10 = f32[128,512]{1,0:T(8,128)} copy(f32[128,512]{1,0:T(8,128)S(1)} %get-tuple-element.2) | data formatting | bytes 524288
  59.2 0.7 %copy.11 = f32[128,512]{1,0:T(8,128)} copy(f32[128,512]{1,0:T(8,128)S(1)} %get-tuple-element.3) | data formatting | bytes 524288

commit v4 on v3

--- a/solution.py
+++ b/solution.py
@@ -15,17 +15,17 @@
 NC = 16
 NH = 8
 PITCH = NC * R + 8
-EARLY = 8
 PIECES = {"": (0, R), "a": (0, R // 2), "b": (R // 2, R // 2)}
 
 SCHEDULE = (
-    "yh", "p0a", "m0b", "xm0", "xp0", "m0a", "p0b", "T", "p1a", "y0", "m1b", "p1b", "m1a", "xp1", "xm1", "T",
-    "xm2b", "p3a", "m3b", "xp2a", "c0", "T", "c2", "p2", "y2", "m2", "xp3a", "xm3b", "T", "c5", "p4a", "T",
-    "c6", "m4b", "m3a", "p3b", "y1", "c3", "T", "c1", "T", "c4", "p5", "T", "c7", (0, -1), "y3", (1, -1),
-    (1, 0), "m5", (2, 1), "q4", (2, -3), "r5", (2, 4), "k2b", "k2a", (2, 3), "q5", "r4", (2, -2), "k1a", "r0b",
-    (1, 2), "q0a", "r1a", "d7", "k1b", "d6", "d5", (0, 2), "u10a", "v10b", "k0b", "q1b", (0, 0), "d4", "u11b",
-    "k0a", "d2", "r1b", "q1a", "v11a", "d3", "k3", "d1", "u11a", "u00a", "r2a", "v11b", "q2b", "v00b", "r2b",
-    "q2a", "v01a", "fa", "u01b", "q3b", "u01a", "r3a", "v01b", "fb", "r3b", "d0", "q3a",
+    "yh", "p0a", "m0b", "xm0", "xp0", "m0a", "p0b", "T", "T", "p1a", "y0", "m1b", "p1b", "m1a", "xp1", "xm1",
+    "T", "T", "xm2b", "p3a", "m3b", "xp2a", "c0", "T", "T", "c2", "p2", "y2", "m2", "xp3a", "xm3b", "T", "T",
+    "c5", "p4a", "T", "T", "c6", "m4b", "m3a", "p3b", "y1", "c3", "T", "T", "c1", "T", "T", "c4", "p5", "T",
+    "T", "c7", (0, -1), "y3", (1, -1), (1, 0), "m5", (2, 1), "q4", (2, -3), "r5", (2, 4), "k2b", "k2a", (2, 3),
+    "q5", "r4", (2, -2), "k1a", "r0b", (1, 2), "q0a", "r1a", "d7", "k1b", "d6", "d5", (0, 2), "u10a", "v10b",
+    "k0b", "q1b", (0, 0), "d4", "u11b", "k0a", "d2", "r1b", "q1a", "v11a", "d3", "k3", "d1", "u11a", "u00a",
+    "r2a", "v11b", "q2b", "v00b", "r2b", "q2a", "v01a", "fa", "u01b", "q3b", "u01a", "r3a", "v01b", "fb", "r3b",
+    "d0", "q3a",
 )
 NEEDS = {
     "p1a": ("p0a",), "p1b": ("p0b",), "m1a": ("m0a",), "m1b": ("m0b",), "p2": ("y0",), "m2": ("y0",),
@@ -54,10 +54,10 @@
 SUMS = {
     "q0": (4, 0), "q1": (3, 0), "q2": (2, 0), "q3": (1, 0), "q4": (1, 1), "q5": (3, 1),
     "r0": (4, 0), "r1": (-3, 0), "r2": (-2, 0), "r3": (-1, 0), "r4": (-1, 1), "r5": (-3, 1),
-    "g0": (4, 1), "g1": (4, 1), "k0": (2, 1), "k1": (-2, 1), "k2": (4, 1), "k3": (0, 1),
+    "k0": (2, 1), "k1": (-2, 1), "k2": (4, 1), "k3": (0, 1),
 }
 SPOTS = ((0, 0), (0, -1), (0, 1), (0, 2), (1, 0), (1, -1), (1, 1), (1, 2))
-X_SPOTS = {"u0": 3, "v0": 3, "u1": 2, "v1": 1, "w": 3}
+X_SPOTS = {"u0": 3, "v0": 3, "u1": 2, "v1": 1}
 COPIES = tuple(n for n in SCHEDULE if isinstance(n, str) and n != "T")
 TILES = tuple(n for n in SCHEDULE if not isinstance(n, str))
 
@@ -78,9 +78,10 @@
 
 
 def kernel(
-    img_ref, txt_ref, codes_ref, scales_ref, scale_ref, bias_ref,
+    img_hbm, txt_hbm, codes_ref, scales_ref, scale_ref, bias_ref,
     dimg_ref, dtxt_ref,
-    codes, scb, pt, J, T, dI, dT, zs, zr, ks, kr, ds_, dr, xs, xr, fs, fr, gs, gr, ws, wr,
+    codes, scb, pt, J, T, dI, dT, zs, zr, ks, kr, ds_, dr, xs, xr, fs, fr,
+    img_ref, txt_ref, in_sem,
     codes_sem, ssem, rsem,
 ):
     bi, ti = lax.axis_index("blk"), lax.axis_index("tile")
@@ -104,35 +105,29 @@
     yhi = {"blk": blk(1 - h, x, k)}
     right, left = {"blk": blk(h, x + 1, k)}, {"blk": blk(h, x - 1, k)}
     core = {"blk": blk(h, x, 1 - k)}
-    across = {"blk": blk(h, x + 2, k)}
-    up_ylo, down_ylo = {"tile": (1 - l) * NZ + zz(1)}, {"tile": (1 - l) * NZ + zz(-1)}
-    partners = [up, down, ylo, yhi, right, left, core]
-    if any(n[0] == "g" for n in COPIES):
-        partners += [up_ylo, down_ylo]
-    if any(n[0] == "w" or n[:2] == "xx" for n in COPIES):
-        partners += [across]
+    partners = (up, down, ylo, yhi, right, left, core)
 
     def codes_copy(r):
         rows = pl.ds(r * R, R)
         return pltpu.make_async_copy(codes_ref.at[rows], codes.at[rows], codes_sem.at[r])
 
+    inputs = [
+        pltpu.make_async_copy(src, dst, in_sem.at[n])
+        for n, (src, dst) in enumerate(((img_hbm, img_ref), (txt_hbm, txt_ref)))
+    ]
+    for c in inputs:
+        c.start()
     barrier = pltpu.get_barrier_semaphore()
     for dev in partners:
         pl.semaphore_signal(barrier, inc=1, device_id=dev, device_id_type=pl.DeviceIdType.MESH)
-    for r in range(NC):
-        codes_copy(r).start()
 
     def landing(name):
         base, rows = split(name)
-        i = int(base[1]) if base[0] in "qrkgduvw" else 0
+        i = int(base[1]) if base[0] in "qrkduv" else 0
         if base[0] in "qr":
             return zs, zr, i if base[0] == "q" else 6 + i, rows
         if base[0] == "k":
             return ks, kr, i, rows
-        if base[0] == "g":
-            return gs, gr, i, rows
-        if base[0] == "w":
-            return ws, wr, i, rows
         if base[0] == "d":
             return ds_, dr, i, rows
         if base[0] == "f":
@@ -144,16 +139,12 @@
         kind = base[0]
         if kind in "pmy" and base != "yh":
             n = int(base[1])
-            dz = {"p": (0, -1, 0, -2, -3, -2, -3), "m": (0, 1, 0, 2, 3, 2, 3), "y": (0, 2, -2, 4)}[kind][n]
+            dz = {"p": (0, -1, 0, -2, -3, -2), "m": (0, 1, 0, 2, 3, 2), "y": (0, 2, -2, 4)}[kind][n]
             spot = J.at[zz(dz), lcol(kind != "y" and n in (2, 5)), rows]
             src, dst, dev = spot, spot, {"p": up, "m": down, "y": ylo}[kind]
-            if n == 6:
-                dev = up_ylo if kind == "p" else down_ylo
         elif kind in "xyc":
             if base == "yh":
                 spot, dev = T.at[bi, rows], yhi
-            elif base[:2] == "xx":
-                spot, dev = T.at[blk(hcol(base == "xx3"), x, k), rows], across
             elif kind == "c":
                 hh, dx = SPOTS[int(base[1])]
                 spot, dev = T.at[blk(hcol(hh), x + dx, k), rows], core
@@ -165,7 +156,7 @@
         else:
             out, into, i, rows = landing(name)
             src, dst = out.at[i, rows], into.at[i, rows]
-            dev = {"g": down_ylo if i else up_ylo, "w": across, "q": up, "r": down, "k": ylo, "d": core, "u": right, "v": left, "f": yhi}[kind]
+            dev = {"q": up, "r": down, "k": ylo, "d": core, "u": right, "v": left, "f": yhi}[kind]
         i = COPIES.index(name)
         return pltpu.make_async_remote_copy(
             src_ref=src, dst_ref=dst, send_sem=ssem.at[i], recv_sem=rsem.at[i], device_id=dev,
@@ -180,16 +171,21 @@
                 seen.add(name)
                 copy(name).wait_recv()
 
+    for c in inputs:
+        c.wait()
+    for r in range(NC):
+        codes_copy(r).start()
     img_unit, _ = unit_rows(img_ref[...].astype(F32))
     J[z, l] = img_unit.astype(BF)
     txt_unit, _ = unit_rows(txt_ref[...].astype(F32))
     T[bi] = txt_unit.astype(BF)
 
-    eye = lax.broadcasted_iota(jnp.int32, (NC, NC), 0) == lax.broadcasted_iota(jnp.int32, (NC, NC), 1)
-    for r in range(NC):
-        row = jnp.broadcast_to(scales_ref[r], (NC, NC))
-        column = jnp.sum(jnp.where(eye, row, 0.0), axis=-1, keepdims=True)
-        scb[r] = jnp.broadcast_to(0.5 * column, (NC, R))
+    def teacher_scales():
+        eye = lax.broadcasted_iota(jnp.int32, (NC, NC), 0) == lax.broadcasted_iota(jnp.int32, (NC, NC), 1)
+        for r in range(NC):
+            row = jnp.broadcast_to(scales_ref[r], (NC, NC))
+            column = jnp.sum(jnp.where(eye, row, 0.0), axis=-1, keepdims=True)
+            scb[r] = jnp.broadcast_to(0.5 * column, (NC, R))
 
     def teacher_rows(r, carry):
         codes_copy(r).wait()
@@ -243,14 +239,14 @@
         base, rows = split(name)
         kind = base[0]
         value = None
-        if kind in "qrkg":
+        if kind in "qrk":
             dz, other = SUMS[base]
             value = dI[zz(dz), lcol(other), rows]
         elif kind == "d":
             hh, dx = SPOTS[int(base[1])]
             value = dT[blk(hcol(hh), x + dx, 1 - k), rows]
-        elif kind in "uvw":
-            value = chip_sum(4 * int(base[1]) + X_SPOTS[kind + base[2:]], rows)
+        elif kind in "uv":
+            value = chip_sum(4 * int(base[1]) + X_SPOTS[kind + base[2]], rows)
         elif kind == "f":
             value = chip_sum(4, rows)
         if value is not None:
@@ -270,9 +266,8 @@
         else:
             events[len(events) - 1].append(item)
 
-    lax.fori_loop(0, EARLY, teacher_rows, 0)
     pl.semaphore_wait(barrier, len(partners))
-    done = EARLY
+    done = 0
     for n, name in enumerate(before):
         if name != "T":
             send(name)
@@ -281,6 +276,8 @@
             while run <= n and before[n - run] == "T":
                 run += 1
             done = first + run
+            if first == 0:
+                teacher_scales()
             lax.fori_loop(first, done, teacher_rows, 0)
 
     def step(s, carry):
@@ -311,6 +308,11 @@
     for name in events[len(TILES)]:
         send(name)
 
+    late = COPIES[-16:]
+    for name in COPIES:
+        if name not in late:
+            copy(name).wait_send()
+
     whole = pl.ds(0, R)
     unit, mag = unit_rows(txt_ref[...].astype(F32))
     arrive(LAST_TEXT)
@@ -324,20 +326,21 @@
     grad = dI[z, l] + arrived("k3", whole) + arrived("q3", whole) + arrived("r3", whole)
     dimg_ref[...] = unit_grad(half_scale * grad, unit, mag)
 
-    for name in COPIES:
+    for name in late:
         copy(name).wait_send()
 
 
 def shards(images, texts, teacher_codes, teacher_scales, student_logit_scale, logit_bias):
     vmem = pl.BlockSpec(memory_space=pltpu.VMEM)
     smem = pl.BlockSpec(memory_space=pltpu.SMEM)
+    hbm = pl.BlockSpec(memory_space=pl.ANY)
     row = lambda *n: pltpu.VMEM((*n, R, E), BF)
     dma = lambda n: pltpu.SemaphoreType.DMA((n,))
     out = pltpu.VMEM((R, E), F32)
     return pl.pallas_call(
         kernel,
         out_shape=(out, out),
-        in_specs=[vmem, vmem, pl.BlockSpec(memory_space=pl.ANY), vmem, smem, smem],
+        in_specs=[hbm, hbm, hbm, vmem, smem, smem],
         out_specs=(vmem, vmem),
         scratch_shapes=[
             pltpu.VMEM((NC * R, NC, R), BF),
@@ -347,7 +350,8 @@
             row(NC),
             pltpu.VMEM((NZ, 2, R, E), F32),
             pltpu.VMEM((NC, R, E), F32),
-            row(12), row(12), row(4), row(4), row(8), row(8), row(8), row(8), row(1), row(1), row(2), row(2), row(2), row(2),
+            row(12), row(12), row(4), row(4), row(8), row(8), row(8), row(8), row(1), row(1),
+            row(), row(), dma(2),
             dma(NC), dma(len(COPIES)), dma(len(COPIES)),
         ],
         compiler_params=pltpu.CompilerParams(

time: 60.3 us -> 58.3 us (0.967)
  Pallas kernels: 56.5 us -> 54.2 us
    pallas_call x1, Pallas kernels: 56.5 us -> 54.2 us  [shards(): pl.pallas_call(kernel, out_shape=(out, out), in_specs=[hbm, hbm, hbm, vme...]
where the time goes in v4:
time: 58.3 us; the launch traced here: 57.6 us
  Pallas kernels  54.2 us (93%)
  between operations  1.93 us (3%)
  local copies, waits for them, and re-layouts  1.41 us (2%)
    pallas_call x1, Pallas kernels, shards(): pl.pallas_call(kernel, out_shape=(out, out), in_specs=[hbm, hbm, hbm, vme...  54.2 us
    unnamed x2, local copies, waits for them, and re-layouts  1.41 us

profile of v4, /device:TPU:2, one launch (start us, length us, event | category | flops | bytes accessed | tf_op | source)
XLA Modules:
  0.0 57.6 jit_solution(9767340820319938643)
XLA Ops:
  1.9 54.2 %shard_map.77 = (f32[128,512]{1,0:T(8,128)S(1)}, f32[128,512]{1,0:T(8,128)S(1)}) custom-call(bf16[128,512]{1,0:T(8,128)(2,1)} %img_hbm.1, bf16[128,512]{1,0:T(8,128)(2,1)} %txt_hbm.1, bf16[2048,16,128]{2,1,0:T(8,128)(2,1)} %codes_ref.1, f32[16,1,16]{2,1,0:T(1,128)} %bitcast.1, f32[1]{0:T(128)S(6)} %copy.12.scale_ref, f32[1]{0:T(128)S(6)} %copy.13.bias_ref), custom_call_target="tpu_custom_call" | custom-call | tf_op jit(solution)/shard_map/pallas_call | solution.py:340
  56.2 0.7 %copy.10 = f32[128,512]{1,0:T(8,128)} copy(f32[128,512]{1,0:T(8,128)S(1)} %get-tuple-element.2) | data formatting | bytes 524288
  56.9 0.7 %copy.11 = f32[128,512]{1,0:T(8,128)} copy(f32[128,512]{1,0:T(8,128)S(1)} %get-tuple-element.3) | data formatting | bytes 524288

commit v5 on v4

--- a/solution.py
+++ b/solution.py
@@ -194,12 +194,12 @@
         dI[r // 2, r % 2] = jnp.zeros((R, E), F32)
 
         def some(g, inner):
-            for u in range(16):
-                i = r * R + g * 16 + u
+            for u in range(32):
+                i = r * R + g * 32 + u
                 pt[pl.ds(i, NC, stride=PITCH), :] = jnp.tanh(codes[i].astype(F32) * sc)
             return inner
 
-        return lax.fori_loop(0, R // 16, some, carry)
+        return lax.fori_loop(0, R // 32, some, carry)
 
     half_scale = 0.5 * scale_ref[0]
     half_bias = 0.5 * bias_ref[0]

time: 58.3 us -> 58.2 us (level)
  no operation moved by 1% of the time
where the time goes in v5:
time: 58.2 us; the launch traced here: 57.6 us
  Pallas kernels  54.3 us (93%)
  between operations  1.93 us (3%)
  local copies, waits for them, and re-layouts  1.41 us (2%)
    pallas_call x1, Pallas kernels, shards(): pl.pallas_call(kernel, out_shape=(out, out), in_specs=[hbm, hbm, hbm, vme...  54.3 us
    unnamed x2, local copies, waits for them, and re-layouts  1.41 us

profile of v5, /device:TPU:2, one launch (start us, length us, event | category | flops | bytes accessed | tf_op | source)
XLA Modules:
  0.0 57.6 jit_solution(6731552030281825844)
XLA Ops:
  1.9 54.3 %shard_map.77 = (f32[128,512]{1,0:T(8,128)S(1)}, f32[128,512]{1,0:T(8,128)S(1)}) custom-call(bf16[128,512]{1,0:T(8,128)(2,1)} %img_hbm.1, bf16[128,512]{1,0:T(8,128)(2,1)} %txt_hbm.1, bf16[2048,16,128]{2,1,0:T(8,128)(2,1)} %codes_ref.1, f32[16,1,16]{2,1,0:T(1,128)} %bitcast.1, f32[1]{0:T(128)S(6)} %copy.12.scale_ref, f32[1]{0:T(128)S(6)} %copy.13.bias_ref), custom_call_target="tpu_custom_call" | custom-call | tf_op jit(solution)/shard_map/pallas_call | solution.py:340
  56.2 0.7 %copy.10 = f32[128,512]{1,0:T(8,128)} copy(f32[128,512]{1,0:T(8,128)S(1)} %get-tuple-element.2) | data formatting | bytes 524288
  56.9 0.7 %copy.11 = f32[128,512]{1,0:T(8,128)} copy(f32[128,512]{1,0:T(8,128)S(1)} %get-tuple-element.3) | data formatting | bytes 524288
